TPU v7x, 32 devices: a whole 2x2x4 slice. The times are simulated.
32 devices in a mesh: seq: 8 (over y, x, core), exp: 4 (over z).
Axes of the slice: x: 2, y: 2, z: 4, core: 2. Of those that a mesh axis runs over, the one named last changes fastest.
Arguments:
- qk_proj: bfloat16 [1024, 2, 2048], P('seq', None, 'exp'), may hold values from -6 to 6
- v_proj: bfloat16 [1024, 4096], P('seq', 'exp'), may hold values from -6 to 6
- z_proj: bfloat16 [1024, 4096], P('seq', 'exp'), may hold values from -6 to 6
- conv_qk: float32 [4, 2, 2048], P(None, None, 'exp'), may hold values from -3 to 3
- conv_v: float32 [4, 4096], P(None, 'exp'), may hold values from -3 to 3
- decay_log: float32 [32, 1024], P('exp', 'seq'), may hold values from -2 to 0
- beta_gate: float32 [32, 1024], P('exp', 'seq'), may hold values from 0.05 to 0.95
- doc_ids: int32 [1024], replicated, may hold values from 0 to 7, never falling along the last dimension, each value on 1 to 256 neighbouring positions
- head_gain: float32 [128], replicated, may hold values from 0.1 to 1.9
- out_weight: bfloat16 [4096, 2048], P('exp'), may hold values from -0.09375 to 0.09375
- residual: bfloat16 [1024, 2048], P(('seq', 'exp')), may hold values from -6 to 6
- post_gain: float32 [2048], replicated, may hold values from 0.1 to 1.9
- route_ids: int32 [1024, 10], P(('seq', 'exp')), may hold values from 0 to 63, all different within a row; in each aligned block of 32 rows (0 to 31, 32 to 63, ...) at most 8 rows name the same one
- route_weight: float32 [1024, 10], P(('seq', 'exp')), may hold values from 0.02 to 0.3
- expert_gate_up: bfloat16 [64, 2, 2048, 512], P(('seq', 'exp')), may hold values from -0.125 to 0.125
- expert_down: bfloat16 [64, 512, 2048], P(('seq', 'exp')), may hold values from -0.25 to 0.25
- shared_gate_up: bfloat16 [2, 2048, 512], replicated, may hold values from -0.125 to 0.125
- shared_down: bfloat16 [512, 2048], replicated, may hold values from -0.25 to 0.25
- shared_gate: float32 [2048], replicated, may hold values from -0.125 to 0.125
Outputs:
- hidden_mid: bfloat16 [1024, 2048], P(('seq', 'exp'))
- moe_out: bfloat16 [1024, 2048], P(('seq', 'exp'))
Inputs may be any that keep to these rules, and one draw needn't show every extreme that they name: `route_ids`: each row names 10 different experts. In each aligned block of 32 rows (the rows of one device) no expert is named by more than 8 rows, and in some blocks an expert is named by exactly 8 rows. `doc_ids`: document numbers never fall along the stream; each document covers 1 to 256 tokens, and one covers exactly 256.
All inputs are finite; a program needn't handle non-finite values.
Results may differ from a plain program's by a relative error of at most 0.0075.
Values may be sent and summed in bfloat16 or wider, within the bound.
A program may use at most 128 MiB of HBM per device.

v0:
```python
import jax
import jax.numpy as jnp
from jax import lax
from jax.sharding import PartitionSpec as P

GROUP = 64


exact_result = lax.Precision.HIGHEST


def shifted(value, axis, by):
    peers = lax.axis_size(axis)
    pairs = [(i, i + by) for i in range(peers) if 0 <= i + by < peers]
    return lax.ppermute(value, axis, pairs)


def entering(part, axis, combine, identity):
    place = lax.axis_index(axis)
    gathered = jax.tree.map(lambda a: lax.all_gather(a, axis), part)
    state = jax.tree.map(lambda a, e: jnp.zeros_like(a) + jnp.asarray(e, a.dtype), part, identity)

    def one(step, state):
        return combine(
            state, jax.tree.map(lambda a: lax.dynamic_index_in_dim(a, step, 0, False), gathered)
        )

    return lax.fori_loop(0, place, one, state)


def causal_conv(extended, weight, doc_window):
    kernel_len = weight.shape[0]
    length = extended.shape[0] - kernel_len + 1
    own_doc = doc_window[kernel_len - 1 :]
    summed = jnp.zeros((length,) + extended.shape[1:], jnp.float32)
    for tap_index in range(kernel_len):
        same_doc = (doc_window[tap_index : tap_index + length] == own_doc).astype(jnp.float32)
        same_doc = same_doc.reshape((length,) + (1,) * (extended.ndim - 1))
        summed = summed + weight[tap_index] * (
            extended[tap_index : tap_index + length].astype(jnp.float32) * same_doc
        )
    return jax.nn.silu(summed)


def prepare(qk_conv, v_conv, decay_log, beta_gate, doc_window, block_len):
    length = v_conv.shape[0]
    head_count = decay_log.shape[0]
    key_heads = head_count // 2
    key_dim = qk_conv.shape[2] // key_heads
    value_dim = v_conv.shape[1] // head_count
    split_qk = qk_conv.reshape(length, 2, key_heads, key_dim)
    unit_qk = split_qk * lax.rsqrt(jnp.sum(split_qk * split_qk, axis=-1, keepdims=True) + 1e-06)
    blocks = length // block_len

    def heads_first(tensor):
        return jnp.transpose(tensor, (1, 0, 2)).reshape(
            head_count, blocks, block_len, tensor.shape[2]
        )

    queries = heads_first(jnp.repeat(unit_qk[:, 0], 2, axis=1) * key_dim ** (-0.5))
    key_vecs = heads_first(jnp.repeat(unit_qk[:, 1], 2, axis=1))
    values = heads_first(v_conv.reshape(length, head_count, value_dim))
    decays = decay_log.reshape(head_count, blocks, block_len)
    rates = beta_gate.reshape(head_count, blocks, block_len)
    kernel_len = doc_window.shape[0] - length + 1
    seg_block = doc_window[kernel_len - 1 :].reshape(blocks, block_len)
    seg_before = doc_window[kernel_len - 2 : kernel_len - 2 + length : block_len]
    return (queries, key_vecs, values, decays, rates, seg_block, seg_before)


def delta_blocks(queries, key_vecs, values, decays, rates, seg_block, seg_before):
    block_len = key_vecs.shape[2]
    value_dim = values.shape[3]
    cum_decay = jnp.cumsum(decays, axis=-1)
    lower_incl = jnp.tril(jnp.ones((block_len, block_len), dtype=bool))
    strict_lower = jnp.tril(jnp.ones((block_len, block_len), dtype=bool), -1)
    same_doc = seg_block[:, :, None] == seg_block[:, None, :]
    keep_mask = same_doc & lower_incl
    spread = cum_decay[..., :, None] - cum_decay[..., None, :]
    within = jnp.exp(jnp.where(keep_mask, spread, 0.0)) * keep_mask
    carried = jnp.exp(cum_decay) * (seg_block == seg_before[:, None])
    key_dots = jnp.einsum("hnik,hnjk->hnij", key_vecs, key_vecs, precision=exact_result)
    system = (
        jnp.eye(block_len, dtype=jnp.float32)
        + rates[..., :, None] * within * key_dots * strict_lower
    )
    right_sides = jnp.concatenate(
        [rates[..., None] * values, (rates * carried)[..., None] * key_vecs], axis=-1
    )
    solved = jax.scipy.linalg.solve_triangular(system, right_sides, lower=True, unit_diagonal=True)
    new_values = solved[..., :value_dim]
    key_weights = solved[..., value_dim:]
    scores = jnp.einsum("hnik,hnjk->hnij", queries, key_vecs, precision=exact_result) * within
    out_local = jnp.einsum("hnij,hnjv->hniv", scores, new_values, precision=exact_result)
    query_eff = carried[..., None] * queries - jnp.einsum(
        "hnij,hnjk->hnik", scores, key_weights, precision=exact_result
    )
    end_keys = within[..., -1, :][..., None] * key_vecs
    transit = carried[..., -1][..., None, None] * jnp.eye(
        key_vecs.shape[3], dtype=jnp.float32
    ) - jnp.einsum("hnjk,hnjl->hnkl", end_keys, key_weights, precision=exact_result)
    offset = jnp.einsum("hnjk,hnjv->hnkv", end_keys, new_values, precision=exact_result)
    return (out_local, query_eff, transit, offset)


def run_blocks(query_eff, out_local, transit, offset, start_state):

    def advance(current_state, pieces):
        effective_query, local_output, permute_matrix, beta_matrix = pieces
        layer_output = (
            jnp.einsum("mjw,mwq->mjq", effective_query, current_state, precision=exact_result)
            + local_output
        )
        following_state = (
            jnp.einsum("jyu,jug->jyg", permute_matrix, current_state, precision=exact_result)
            + beta_matrix
        )
        return (following_state, layer_output)

    stacked = (
        jnp.moveaxis(query_eff, 1, 0),
        jnp.moveaxis(out_local, 1, 0),
        jnp.moveaxis(transit, 1, 0),
        jnp.moveaxis(offset, 1, 0),
    )
    last_state, outputs = lax.scan(advance, start_state, stacked)
    return outputs


def gated_norm(outputs, z_proj, head_gain):
    blocks, head_count, block_len, value_dim = outputs.shape
    attn_heads = jnp.transpose(outputs, (0, 2, 1, 3)).reshape(
        blocks * block_len, head_count, value_dim
    )
    gate_z = z_proj.reshape(blocks * block_len, head_count, value_dim).astype(jnp.float32)
    scaled = (
        attn_heads
        * lax.rsqrt(jnp.mean(attn_heads * attn_heads, axis=-1, keepdims=True) + 1e-06)
        * head_gain
        * jax.nn.silu(gate_z)
    )
    return scaled.reshape(blocks * block_len, head_count * value_dim).astype(jnp.bfloat16)


def rms_scale(hidden, gain):
    return (
        hidden * lax.rsqrt(jnp.mean(hidden * hidden, axis=-1, keepdims=True) + 1e-06) * gain
    ).astype(jnp.bfloat16)


def compose(initial_mapping, secondary_mapping):
    return (
        jnp.einsum(
            "hkl,hlm->hkm", secondary_mapping[0], initial_mapping[0], precision=exact_result
        ),
        jnp.einsum("jyu,jug->jyg", secondary_mapping[0], initial_mapping[1], precision=exact_result)
        + secondary_mapping[1],
    )


def experts_apply(received, expert_gate_up, expert_down):
    gate_up = jnp.einsum(
        "secd,ezdf->zsecf", received, expert_gate_up, preferred_element_type=jnp.float32
    )
    activated = (jax.nn.silu(gate_up[0]) * gate_up[1]).astype(jnp.bfloat16)
    return jnp.einsum(
        "secf,efd->secd", activated, expert_down, preferred_element_type=jnp.float32
    ).astype(jnp.bfloat16)


def shards(
    qk_proj,
    v_proj,
    z_proj,
    conv_qk,
    conv_v,
    decay_log,
    beta_gate,
    doc_ids,
    head_gain,
    out_weight,
    residual,
    post_gain,
    route_ids,
    route_weight,
    expert_gate_up,
    expert_down,
    shared_gate_up,
    shared_down,
    shared_gate,
):
    kernel_len = conv_qk.shape[0]
    length = qk_proj.shape[0]
    key_cols = qk_proj.shape[2]
    flat_qk = qk_proj.reshape(length, 2 * key_cols)
    rim_send = jnp.concatenate(
        [flat_qk[length - kernel_len + 1 :], v_proj[length - kernel_len + 1 :]], axis=1
    )
    rim_recv = shifted(rim_send, "seq", 1)
    doc_pad = jnp.concatenate([jnp.full((kernel_len - 1,), -1, jnp.int32), doc_ids])
    doc_window = lax.dynamic_slice_in_dim(
        doc_pad, lax.axis_index("seq") * length, length + kernel_len - 1
    )
    qk_ext = jnp.concatenate(
        [rim_recv[:, : 2 * key_cols].reshape(kernel_len - 1, 2, key_cols), qk_proj], axis=0
    )
    v_ext = jnp.concatenate([rim_recv[:, 2 * key_cols :], v_proj], axis=0)
    qk_conv = causal_conv(qk_ext, conv_qk, doc_window)
    v_conv = causal_conv(v_ext, conv_v, doc_window)
    queries, key_vecs, values, decays, rates, seg_block, seg_before = prepare(
        qk_conv, v_conv, decay_log, beta_gate, doc_window, GROUP
    )
    out_local, query_eff, transit, offset = delta_blocks(
        queries, key_vecs, values, decays, rates, seg_block, seg_before
    )
    head_count = transit.shape[0]
    key_dim = transit.shape[2]
    identity = jnp.broadcast_to(jnp.eye(key_dim, dtype=jnp.float32), (head_count, key_dim, key_dim))
    zero_state = jnp.zeros((head_count, key_dim, offset.shape[3]), jnp.float32)

    def fold_block(carried_map, pieces):
        return (compose(carried_map, pieces), None)

    device_map, unused = lax.scan(
        fold_block,
        (identity, zero_state),
        (jnp.moveaxis(transit, 1, 0), jnp.moveaxis(offset, 1, 0)),
    )
    device_transfer, device_offset = device_map
    prefix = entering((device_transfer, device_offset), "seq", compose, (identity, zero_state))
    start_state = prefix[1]
    outputs = run_blocks(query_eff, out_local, transit, offset, start_state)
    gated = gated_norm(outputs, z_proj, head_gain)
    attn_part = lax.psum_scatter(
        jnp.dot(gated, out_weight, preferred_element_type=jnp.float32),
        "exp",
        scatter_dimension=0,
        tiled=True,
    )
    hidden = residual.astype(jnp.float32) + attn_part
    normed = rms_scale(hidden, post_gain)
    row_count = normed.shape[0]
    model_width = normed.shape[1]
    top_count = route_ids.shape[1]
    exp_dev = expert_down.shape[0]
    seq_count = lax.axis_size("seq")
    exp_count = lax.axis_size("exp")
    experts_all = exp_dev * seq_count * exp_count
    capacity = max(2, (row_count * top_count * 8 + 5 * experts_all - 1) // (5 * experts_all))
    pair_total = row_count * top_count
    flat_ids = route_ids.reshape(-1)
    pair_index = jnp.arange(pair_total, dtype=jnp.int32)
    earlier = (flat_ids[:, None] == flat_ids[None, :]) & (pair_index[None, :] < pair_index[:, None])
    slot_rank = jnp.sum(earlier.astype(jnp.int32), axis=1)
    dest_slot = flat_ids * capacity + slot_rank
    send_rows = (
        jnp.zeros((experts_all * capacity, model_width), jnp.bfloat16)
        .at[dest_slot]
        .set(jnp.repeat(normed, top_count, axis=0))
    )
    send_four = send_rows.reshape(seq_count * exp_count, exp_dev, capacity, model_width)
    returned = lax.all_to_all(
        experts_apply(
            lax.all_to_all(send_four, ("seq", "exp"), split_axis=0, concat_axis=0, tiled=True),
            expert_gate_up,
            expert_down,
        ),
        ("seq", "exp"),
        split_axis=0,
        concat_axis=0,
        tiled=True,
    )
    picked = returned.reshape(experts_all * capacity, model_width)[dest_slot].reshape(
        row_count, top_count, model_width
    )
    weighted = jnp.sum(route_weight[..., None] * picked.astype(jnp.float32), axis=1)
    shared_both = jnp.einsum(
        "rd,zdf->zrf", normed, shared_gate_up, preferred_element_type=jnp.float32
    )
    shared_act = (jax.nn.silu(shared_both[0]) * shared_both[1]).astype(jnp.bfloat16)
    shared_branch = jnp.dot(shared_act, shared_down, preferred_element_type=jnp.float32)
    shared_scale = jax.nn.sigmoid(
        jnp.dot(normed.astype(jnp.float32), shared_gate, precision=exact_result)
    )
    moe_sum = weighted + shared_scale[:, None] * shared_branch
    return (hidden.astype(jnp.bfloat16), moe_sum.astype(jnp.bfloat16))


def solution(mesh):
    placed = (
        P("seq", None, "exp"),
        P("seq", "exp"),
        P("seq", "exp"),
        P(None, None, "exp"),
        P(None, "exp"),
        P("exp", "seq"),
        P("exp", "seq"),
        P(),
        P(),
        P("exp", None),
        P(("seq", "exp"), None),
        P(),
        P(("seq", "exp"), None),
        P(("seq", "exp"), None),
        P(("seq", "exp"), None, None, None),
        P(("seq", "exp"), None, None),
        P(),
        P(),
        P(),
    )
    return jax.shard_map(
        shards,
        mesh=mesh,
        in_specs=placed,
        out_specs=(P(("seq", "exp"), None), P(("seq", "exp"), None)),
        check_vma=False,
    )
```

profile of v0, /device:TPU:24, one launch (start us, length us, event | category | flops | bytes accessed | tf_op | source)
XLA Modules:
  0.0 416.5 jit_solution(14695107215026658902)
XLA Ops:
  7.2 0.8 slice_bitcast_fusion.5
  8.1 0.7 slice.122
  8.8 1.7 collective-permute-start
  10.6 0.8 pad_dynamic-slice_fusion
  11.6 0.6 fusion.92
  12.2 0.7 slice_bitcast_fusion.9
  13.1 0.8 reshape.224
  14.3 1.5 fusion.100
  16.0 0.8 mul.419
  16.7 0.7 iota_compare_fusion.4
  18.4 0.7 copy.116
  19.7 1.2 constant_dynamic-update-slice_fusion
  20.9 2.4 divide_multiply_fusion
  25.1 1.8 fusion.46
  26.9 79.4 %custom-call.4 = f32[8,2,1,64,64]{3,4,2,1,0:T(8,128)S(1)} custom-call(f32[8,2,1,64,64]{4,3,2,1,0:T(8,128)} %fusion.46), custom_call_target="InvertDiagBlocksLowerTriangular" | custom-call | tf_op jit(solution)/shard_map/jit(_solve_triangular)/vmap(vmap())/triangular_solve | solution.py:90
  106.3 2.1 copy_bitcast_fusion
  108.4 1.0 broadcast_multiply_fusion
  109.4 1.0 fusion.53
  110.5 2.0 convolution_bitcast_fusion
  112.5 1.1 copy.125
  113.7 2.0 fusion.40
  115.8 0.9 broadcast_in_dim.31
  116.6 10.2 %while.39 = (s32[]{:T(128)}, f32[8,128,128]{2,1,0:T(8,128)}, f32[8,128,128]{2,1,0:T(8,128)}, f32[2,8,128,128]{3,2,1,0:T(8,128)S(1)}, f32[2,8,128,128]{3,2,1,0:T(8,128)}, /*index=5*/s32[]{:T(128)}, s32[]{:T(128)}) while((s32[]{:T(128)}, f32[8,128,128]{2,1,0:T(8,128)}, f32[8,128,128]{2,1,0:T(8,128)}, ...), condition=%wide.region_3.4_spmd.clone, body=%wide.region_2.3_spmd.clone.sunk | while | flops 402915328 | bytes 7865463 | solution.py:224
  116.6 1.1 copy.205
  117.7 2.5 convolution_add_fusion.9
  120.2 1.5 fusion.141
  121.8 1.1 copy.205
  122.9 2.5 convolution_add_fusion.9
  125.4 1.5 fusion.141
  126.9 0.7 all-gather.7.cloned.1.call-update
  127.8 2.1 convolution_multiply_fusion.1
  129.9 1.5 convolution_bitcast_fusion.2
  131.4 1.5 fusion.41
  132.9 32.4 %all-gather.5.cloned.1.call-done = f32[64,128,128]{2,1,0:T(8,128)} async-done(((f32[8,128,128]{2,1,0:T(8,128)}), f32[64,128,128]{2,1,0:T(8,128)}) %all-gather.5.cloned.1.call-update) | async-done | bytes 4194320 | tf_op jit(solution)/shard_map/all_gather | solution.py:20
  165.2 38.6 %all-gather.7.cloned.1.call-done = f32[64,128,128]{2,1,0:T(8,128)} async-done(((f32[8,128,128]{2,1,0:T(8,128)}), f32[64,128,128]{2,1,0:T(8,128)}) %all-gather.7.cloned.1.call-update) | async-done | bytes 4194320 | tf_op jit(solution)/shard_map/all_gather | solution.py:20
  203.9 0.9 broadcast_in_dim.30
  204.7 9.9 %while.38 = (s32[]{:T(128)}, f32[8,128,128]{2,1,0:T(8,128)}, f32[2,8,64,128]{3,2,1,0:T(8,128)}, f32[2,8,128,128]{3,2,1,0:T(8,128)S(1)}, f32[2,8,128,128]{3,2,1,0...) while((s32[]{:T(128)}, f32[8,128,128]{2,1,0:T(8,128)}, ...), condition=%wide.region_7.8_spmd, body=%wide.region_6.7_spmd.sunk | while | flops 302186496 | bytes 8652913 | solution.py:126
  204.7 1.1 copy.203
  205.9 2.3 fusion.136
  208.2 1.5 convolution_add_fusion.8
  209.7 1.1 copy.203
  210.8 2.3 fusion.136
  213.1 1.5 convolution_add_fusion.8
  214.6 1.3 multiply_reduce_fusion.1
  216.0 1.4 copy.132
  217.6 4.1 fusion.77
  222.4 50.1 %reduce-scatter.2.cloned.1.call-done = f32[32,2048]{1,0:T(8,128)} async-done(((f32[128,2048]{1,0:T(8,128)}), f32[32,2048]{1,0:T(8,128)}) %reduce-scatter.2.cloned.1.call-update) | async-done | bytes 262160 | tf_op jit(solution)/shard_map/reduce_scatter | solution.py:234
  272.5 1.1 multiply_reduce_fusion.3
  273.6 1.6 multiply_convert_fusion
  275.3 1.6 broadcast_in_dim.38
  276.9 2.5 reshape.250
  279.4 4.1 scatter_custom_fusion
  283.5 53.0 %all_to_all.10 = bf16[32,2,8,2048]{3,2,1,0:T(8,128)(2,1)S(1)} all-to-all(bf16[32,2,8,2048]{3,2,1,0:T(8,128)(2,1)} %bitcast.224), channel_id=1, replica_groups=mesh['seq'=8,'exp'=4] {'seq','exp'}, dimensions={0} | all-to-all | bytes 4194304 | tf_op jit(solution)/shard_map/all_to_all | solution.py:264
  336.4 5.9 %fusion.35 = f32[2,32,2,8,512]{4,3,0,1,2:T(8,128)S(1)} fusion(bf16[2,2,2048,512]{3,2,1,0:T(8,128)(2,1)} %param.39, bf16[32,2,8,2048]{3,2,1,0:T(8,128)(2,1)S(1)} %all_to_all.10), kind=kOutput, calls=%fused_computation.39 | convolution fusion | flops 2147483648 | bytes 12582912 | tf_op jit(solution)/shard_map/secd,ezdf->zsecf/dot_general | solution.py:162
  342.4 1.3 fusion.29
  343.7 1.4 copy.140
  345.1 4.9 %all-to-all-start.1 = ((bf16[32,2,8,2048]{3,2,1,0:T(8,128)(2,1)}), bf16[32,2,8,2048]{3,2,1,0:T(8,128)(2,1)}, u32[]{:S(2)}, u32[]{:S(2)}) async-start(bf16[32,2,8,2048]{3,2,1,0:T(8,128)(2,1)} %copy.140), calls=%async_computation.2 | async-start | bytes 4194304 | tf_op jit(solution)/shard_map/all_to_all | solution.py:262
  350.8 0.7 fusion.50
  351.5 3.6 convolution_bitcast_fusion.3
  355.2 41.5 %all-to-all-done.1 = bf16[32,2,8,2048]{3,2,1,0:T(8,128)(2,1)} async-done(((bf16[32,2,8,2048]{3,2,1,0:T(8,128)(2,1)}), bf16[32,2,8,2048]{3,2,1,0:T(8,128)(2,1)}, u32[]{:S(2)}, u32[]{:S(2)}) %all-to-all-start.1) | async-done | bytes 2097184 | tf_op jit(solution)/shard_map/all_to_all | solution.py:262
  396.7 6.4 %gather_fusion = bf16[320,2048]{1,0:T(8,128)(2,1)S(1)} fusion(bf16[512,2048]{1,0:T(8,128)(2,1)} %bitcast.52, s32[1024]{0:T(1024)} %pad_clamp_fusion), kind=kCustom, calls=%fused_computation | custom fusion | bytes 2622720 | tf_op jit(solution)/shard_map/gather | solution.py:273
  403.0 2.1 reshape.237
  405.2 3.7 multiply_reduce_fusion
  408.9 1.1 fusion.33
  (128 shorter events, 6.3 us)
Async XLA Ops:
  7.2 401.7 %copy-start = (bf16[512,2048]{1,0:T(8,128)(2,1)S(1)}, bf16[512,2048]{1,0:T(8,128)(2,1)}, u32[]{:S(2)}) copy-start(bf16[512,2048]{1,0:T(8,128)(2,1)} %param.42) | copy-start | bytes 6291460
  7.2 158.1 %all-gather.5.cloned.1.call-start = ((), (), s32[]{:S(2)}) async-start(), calls=%async_computation.4 | async-start | bytes 4718592 | tf_op jit(solution)/shard_map/all_gather | solution.py:20
  8.8 10.3 %collective-permute-start = (bf16[3,2048]{1,0:T(4,128)(2,1)S(1)}, bf16[3,2048]{1,0:T(4,128)(2,1)S(1)}, u32[]{:S(2)}, u32[]{:S(2)}) collective-permute-start(bf16[3,2048]{1,0:T(4,128)(2,1)S(1)} %pad_maximum_fusion.1), channel_id=1, source_target_pairs={{0,4},{4,8},{8,12},{12,16},{16,20},{20,24},{24,28},{1,5},{5,9},{9,... | collective-permute-start | bytes 36872 | tf_op jit(solution)/shard_map/ppermute | solution.py:15
  11.4 12.4 %copy-start.25 = (f32[128]{0:T(128)}, f32[128]{0:T(128)S(1)}, u32[]{:S(2)}) copy-start(f32[128]{0:T(128)S(1)} %get-tuple-element.245) | copy-start | bytes 1540
  11.4 12.5 %copy-start.26 = (f32[128]{0:T(128)}, f32[128]{0:T(128)S(1)}, u32[]{:S(2)}) copy-start(f32[128]{0:T(128)S(1)} %get-tuple-element.246) | copy-start | bytes 1540
  11.4 12.5 %copy-start.27 = (f32[128]{0:T(128)}, f32[128]{0:T(128)S(1)}, u32[]{:S(2)}) copy-start(f32[128]{0:T(128)S(1)} %get-tuple-element.247) | copy-start | bytes 1540
  15.9 5.0 %copy-start.8 = (pred[2,64,64]{2,1,0:T(8,128)(4,1)}, pred[2,64,64]{2,1,0:T(8,128)(4,1)S(1)}, u32[]{:S(2)}) copy-start(pred[2,64,64]{2,1,0:T(8,128)(4,1)S(1)} %get-tuple-element.243) | copy-start | bytes 24580
  16.7 0.7 copy-start.11
  17.4 3.5 copy-start.13
  23.9 1.1 copy-start.9
  23.9 1.1 copy-start.12
  23.9 1.1 copy-start.15
  23.9 1.1 copy-start.16
  23.9 1.1 copy-start.18
  23.9 1.1 copy-start.22
  25.0 88.6 %copy-start.3 = (f32[128,4,2,128]{3,0,2,1:T(8,128)}, f32[128,4,2,128]{3,0,2,1:T(8,128)S(1)}, u32[]{:S(2)}) copy-start(f32[128,4,2,128]{3,0,2,1:T(8,128)S(1)} %broadcast_in_dim.34) | copy-start | bytes 1572868
  110.5 3.2 copy-start.4
  110.5 3.2 copy-start.19
  116.6 11.1 %copy-start.14 = (f32[8,2,64]{2,0,1:T(8,128)S(1)}, f32[8,2,64]{2,0,1:T(8,128)}, u32[]{:S(2)}) copy-start(f32[8,2,64]{2,0,1:T(8,128)} %copy-done.13) | copy-start | bytes 12292
  116.6 11.1 %copy-start.28 = (f32[128]{0:T(128)S(1)}, f32[128]{0:T(128)}, u32[]{:S(2)}) copy-start(f32[128]{0:T(128)} %param.33) | copy-start | bytes 1540
  116.6 3.6 copy-start.2
  121.7 3.6 copy-start.2
  126.9 1.0 copy-start.10
  126.9 77.0 %all-gather.7.cloned.1.call-start = ((), (), s32[]{:S(2)}) async-start(), calls=%async_computation.5 | async-start | bytes 4718592 | tf_op jit(solution)/shard_map/all_gather | solution.py:20
  127.6 144.9 %reduce-scatter.2.cloned.1.call-start = ((), (), s32[]{:S(2)}) async-start(), calls=%async_computation.3 | async-start | bytes 1310720 | tf_op jit(solution)/shard_map/reduce_scatter | solution.py:234
  127.7 2.2 copy-start.5
  204.7 3.5 copy-start.1
  209.7 3.5 copy-start.1
  214.6 3.0 copy-start.31
  217.6 4.2 %copy-start.17 = (s32[32,10]{0,1:T(8,128)S(1)}, s32[32,10]{0,1:T(8,128)}, u32[]{:S(2)}) copy-start(s32[32,10]{0,1:T(8,128)} %param.37) | copy-start | bytes 3844
  217.6 55.0 %copy-start.7 = (bf16[32,2048]{1,0:T(8,128)(2,1)S(1)}, bf16[32,2048]{1,0:T(8,128)(2,1)}, u32[]{:S(2)}) copy-start(bf16[32,2048]{1,0:T(8,128)(2,1)} %param.35) | copy-start | bytes 393220
  217.6 56.0 %copy-start.20 = (f32[2048]{0:T(1024)S(1)}, f32[2048]{0:T(1024)}, u32[]{:S(2)}) copy-start(f32[2048]{0:T(1024)} %param.36) | copy-start | bytes 24580
  222.4 57.0 %copy-start.23 = (s32[320]{0:T(512)}, s32[320]{0:T(512)S(1)}, u32[]{:S(2)}) copy-start(s32[320]{0:T(512)S(1)} %fusion.93) | copy-start | bytes 3844
  336.4 5.9 %copy-start.30 = (bf16[2,512,2048]{2,1,0:T(8,128)(2,1)S(1)}, bf16[2,512,2048]{2,1,0:T(8,128)(2,1)}, u32[]{:S(2)}) copy-start(bf16[2,512,2048]{2,1,0:T(8,128)(2,1)} %param.40) | copy-start | bytes 12582916
  345.1 5.0 %copy-start.21 = (f32[32,10]{0,1:T(8,128)S(1)}, f32[32,10]{0,1:T(8,128)}, u32[]{:S(2)}) copy-start(f32[32,10]{0,1:T(8,128)} %param.38) | copy-start | bytes 3844
  345.1 5.0 %copy-start.24 = (s32[320]{0:T(512)S(1)}, s32[320]{0:T(512)}, u32[]{:S(2)}) copy-start(s32[320]{0:T(512)} %copy-done.23) | copy-start | bytes 3844
  345.1 5.7 %copy-start.32 = (f32[2048]{0:T(1024)S(1)}, f32[2048]{0:T(1024)}, u32[]{:S(2)}) copy-start(f32[2048]{0:T(1024)} %param.43) | copy-start | bytes 24580
  345.1 51.5 %all-to-all-start.1 = ((bf16[32,2,8,2048]{3,2,1,0:T(8,128)(2,1)}), bf16[32,2,8,2048]{3,2,1,0:T(8,128)(2,1)}, u32[]{:S(2)}, u32[]{:S(2)}) async-start(bf16[32,2,8,2048]{3,2,1,0:T(8,128)(2,1)} %copy.140), calls=%async_computation.2 | async-start | bytes 4194304 | tf_op jit(solution)/shard_map/all_to_all | solution.py:262
  405.2 3.7 copy-start.6
  405.2 3.7 copy-start.29
Sparse Core Ops, SparseCore 0:
  127.0 38.1 all-gather.4
  167.1 36.7 all-gather.6
  221.9 50.6 reduce-scatter.1
where the time goes:
time: 421 us; the launch traced here: 417 us
  waiting for transfers between devices  163 us (39%)
  other arithmetic  96.7 us (23%)
  blocking collectives  53 us (13%)
  matrix products  44.2 us (10%)
  local copies, waits for them, and re-layouts  38.1 us (9%)
  between operations  14.4 us (3%)
  starting transfers between devices  6.8 us (2%)
    another operation x4, other arithmetic, delta_blocks(): jax.scipy.linalg.solve_triangular(system, right_sides, lower=True, unit_d...  80.7 us
    all_gather x2, waiting for transfers between devices, entering(): gathered = jax.tree.map(lambda a: lax.all_gather(a, axis), part)  71 us
    all_to_all x1, blocking collectives, shards(): lax.all_to_all(send_four, ('seq', 'exp'), split_axis=0, concat_axis=0, ti...  53 us
    reduce_scatter x1, waiting for transfers between devices, shards(): lax.psum_scatter(jnp.dot(gated, out_weight, preferred_element_type=jnp.fl...  50.1 us
    all_to_all x1, waiting for transfers between devices, shards(): lax.all_to_all(experts_apply(lax.all_to_all(send_four, ('seq', 'exp'), sp...  41.5 us
  transfers between devices with their start and end apart: 5, of which 4 were waited for; matrix products, arithmetic and copies ran while one was open for 5% of the time, Pallas kernels for 0%

commit v1 on v0

v1 whole, which is shorter than its diff:
```python
import functools

import jax
import jax.numpy as jnp
from jax import lax
from jax.experimental import pallas as pl
from jax.experimental.pallas import tpu as pltpu
from jax.sharding import PartitionSpec as P

exact = lax.Precision.HIGHEST
f32 = jnp.float32
bf16 = jnp.bfloat16
RIM = 8


def dot(a, b, dims=((1,), (0,))):
    return lax.dot_general(
        a.astype(bf16), b.astype(bf16), (dims, ((), ())), preferred_element_type=f32
    )


def dot_exact(a, b, dims=((1,), (0,))):
    return lax.dot_general(a, b, (dims, ((), ())), precision=exact, preferred_element_type=f32)


def silu(x):
    return x * jax.nn.sigmoid(x)


def shifted(value, axis, by):
    peers = lax.axis_size(axis)
    pairs = [(i, i + by) for i in range(peers) if 0 <= i + by < peers]
    return lax.ppermute(value, axis, pairs)


def unit_lower_inverse(lower, row, col):
    size = lower.shape[0]
    inverse = jnp.where(row == col, 1.0, jnp.where(row // 2 == col // 2, -lower, 0.0))
    span = 2
    while span < size:
        joins = (row // (2 * span) == col // (2 * span)) & (row // span != col // span)
        corner = jnp.where(joins, lower, 0.0)
        inverse = inverse - dot(dot(inverse, corner), inverse)
        span *= 2
    return inverse


def conv_silu(prev, own, taps, masks):
    length = own.shape[0]
    ext = jnp.concatenate([prev, own], axis=0).astype(f32)
    kernel_len = taps.shape[0]
    total = taps[kernel_len - 1 : kernel_len] * ext[RIM:]
    for i in range(kernel_len - 1):
        at = RIM - (kernel_len - 1) + i
        total = total + taps[i : i + 1] * (ext[at : at + length] * masks[:, i : i + 1])
    return silu(total)


def delta_kernel(
    qk_ref, v_ref, rim_ref, taps_qk_ref, taps_v_ref, decay_ref, beta_ref, cols_ref, row_ref,
    out_ref, query_ref, move_ref, add_ref,
):
    length = v_ref.shape[0]
    heads = decay_ref.shape[0]
    dim = v_ref.shape[1] // heads
    key_cols = taps_qk_ref.shape[1] // 2
    row = lax.broadcasted_iota(jnp.int32, (length, length), 0)
    col = lax.broadcasted_iota(jnp.int32, (length, length), 1)
    masks = cols_ref[...]
    doc_col = masks[:, 4:5]
    enters = masks[:, 5:6]
    doc_row = row_ref[0:1, :]
    keep = (row >= col) & (doc_col == doc_row)
    keep_f = keep.astype(f32)
    strict = jnp.where(row > col, keep_f, 0.0)
    decay = decay_ref[...]
    cum_row = dot_exact(decay, (row <= col).astype(f32))
    cum_col = dot_exact((row >= col).astype(f32), decay, ((1,), (1,)))
    beta_col = dot_exact((row == col).astype(f32), beta_ref[...], ((1,), (1,)))
    ends = (doc_col == doc_col[length - 1 : length]).astype(f32)
    eye = (row == col).astype(f32)

    def head_cols(ref, rim_at, taps_ref, at):
        return conv_silu(
            rim_ref[:, rim_at + at : rim_at + at + dim],
            ref[:, at : at + dim],
            taps_ref[:, at : at + dim],
            masks,
        )

    for j in range(heads // 2):
        q = head_cols(qk_ref, 0, taps_qk_ref, j * dim)
        k = head_cols(qk_ref, 0, taps_qk_ref, key_cols + j * dim)
        q = q * (lax.rsqrt(jnp.sum(q * q, axis=1, keepdims=True) + 1e-06) * dim ** (-0.5))
        k = k * lax.rsqrt(jnp.sum(k * k, axis=1, keepdims=True) + 1e-06)
        both = dot_exact(jnp.concatenate([q, k], axis=0), k, ((1,), (1,)))
        qk, kk = both[:length], both[length:]
        for h in (2 * j, 2 * j + 1):
            v = head_cols(v_ref, 2 * key_cols, taps_v_ref, h * dim)
            spread = cum_col[:, h : h + 1] - cum_row[h : h + 1, :]
            within = jnp.exp(jnp.where(keep, spread, 0.0)) * keep_f
            carried = jnp.exp(cum_col[:, h : h + 1]) * enters
            beta = beta_col[:, h : h + 1]
            inverse = unit_lower_inverse(beta * within * kk * strict, row, col)
            solved = dot(
                inverse, jnp.concatenate([beta * v, (beta * carried) * k], axis=1)
            ).astype(bf16)
            local = dot(qk * within, solved)
            last = cum_col[length - 1 : length, h : h + 1]
            to_end = jnp.exp((last - cum_col[:, h : h + 1]) * ends) * ends
            end = dot(to_end * k, solved, ((0,), (0,)))
            out_ref[h] = local[:, :dim]
            query_ref[h] = (carried * q - local[:, dim:]).astype(bf16)
            add_ref[h] = end[:, :dim]
            move_ref[h] = (carried[length - 1 : length] * eye - end[:, dim:]).astype(bf16)


def project_kernel(query_ref, out_ref, state_ref, z_ref, gain_ref, weight_ref, part_ref):
    heads, length, dim = out_ref.shape
    gated = []
    for h in range(heads):
        attn = out_ref[h] + dot(query_ref[h], state_ref[h])
        scale = lax.rsqrt(jnp.mean(attn * attn, axis=1, keepdims=True) + 1e-06)
        z = z_ref[:, h * dim : (h + 1) * dim].astype(f32)
        gated.append((attn * scale * gain_ref[...] * silu(z)).astype(bf16))
    part_ref[...] = dot(jnp.concatenate(gated, axis=1), weight_ref[...])


def expert_kernel(rows_ref, share_ref, up_ref, down_ref, out_ref):
    total = None
    for e in range(up_ref.shape[0]):
        gate = dot(rows_ref[...], up_ref[e, 0])
        up = dot(rows_ref[...], up_ref[e, 1])
        act = (silu(gate) * up).astype(bf16)
        term = share_ref[:, e : e + 1] * dot(act, down_ref[e])
        total = term if total is None else total + term
    out_ref[...] = total


def params(**more):
    return pltpu.CompilerParams(vmem_limit_bytes=56 * 1024 * 1024, **more)


VM = pl.BlockSpec(memory_space=pltpu.VMEM)


def shards(
    qk_proj, v_proj, z_proj, conv_qk, conv_v, decay_log, beta_gate, doc_ids, head_gain,
    out_weight, residual, post_gain, route_ids, route_weight, expert_gate_up, expert_down,
    shared_gate_up, shared_down, shared_gate,
):
    kernel_len = conv_qk.shape[0]
    length = qk_proj.shape[0]
    key_cols = qk_proj.shape[2]
    heads = decay_log.shape[0]
    dim = v_proj.shape[1] // heads
    width = residual.shape[1]
    seq_count = lax.axis_size("seq")
    place = lax.axis_index("seq")
    me = place * lax.axis_size("exp") + lax.axis_index("exp")
    exp_dev = expert_down.shape[0]

    own_share = jnp.sum(
        jnp.where(
            route_ids[:, :, None] == jnp.arange(exp_dev * seq_count * lax.axis_size("exp")),
            route_weight[:, :, None],
            0.0,
        ),
        axis=1,
    )
    shares = lax.all_gather(own_share, ("seq", "exp"), axis=0, tiled=True)
    shares = lax.dynamic_slice_in_dim(shares, me * exp_dev, exp_dev, axis=1)

    flat_qk = qk_proj.reshape(length, 2 * key_cols)
    rim = shifted(
        jnp.concatenate([flat_qk[length - RIM :], v_proj[length - RIM :]], axis=1), "seq", 1
    )
    pad = kernel_len - 1
    doc_pad = jnp.concatenate([jnp.full((pad,), -1, jnp.int32), doc_ids])
    window = lax.dynamic_slice_in_dim(doc_pad, place * length, length + pad)
    own_doc = window[pad:]
    cols = [(window[i : i + length] == own_doc).astype(f32) for i in range(pad)]
    cols += [jnp.zeros((length,), f32)] * (4 - pad)
    cols += [own_doc.astype(f32), (own_doc == window[pad - 1]).astype(f32)]
    cols = jnp.stack(cols, axis=1)
    out_local, query, move, add = pl.pallas_call(
        delta_kernel,
        out_shape=(
            jax.ShapeDtypeStruct((heads, length, dim), f32),
            jax.ShapeDtypeStruct((heads, length, dim), bf16),
            jax.ShapeDtypeStruct((heads, dim, dim), bf16),
            jax.ShapeDtypeStruct((heads, dim, dim), f32),
        ),
        in_specs=[VM] * 9,
        out_specs=(VM,) * 4,
        compiler_params=params(),
        name="delta",
    )(
        flat_qk, v_proj, rim, conv_qk.reshape(kernel_len, 2 * key_cols), conv_v, decay_log,
        beta_gate, cols, own_doc.astype(f32).reshape(1, length),
    )
    state = add
    for _ in range(max(1, seq_count // 4) - 1):
        before = shifted(state.astype(bf16), "seq", 1)
        state = add + jnp.einsum("hkl,hlv->hkv", move, before, preferred_element_type=f32)
    start = shifted(state.astype(bf16), "seq", 1)
    part = pl.pallas_call(
        project_kernel,
        out_shape=jax.ShapeDtypeStruct((length, width), f32),
        in_specs=[VM] * 6,
        out_specs=VM,
        compiler_params=params(),
        name="project",
    )(query, out_local, start, z_proj, head_gain.reshape(1, dim), out_weight)
    attn_part = lax.psum_scatter(part, "exp", scatter_dimension=0, tiled=True)
    hidden = residual.astype(f32) + attn_part
    normed = (
        hidden * lax.rsqrt(jnp.mean(hidden * hidden, axis=-1, keepdims=True) + 1e-06) * post_gain
    ).astype(bf16)
    gathered = lax.all_gather(normed, ("seq", "exp"), axis=0, tiled=True)
    tokens = gathered.shape[0]
    tile = 256
    parts = pl.pallas_call(
        expert_kernel,
        out_shape=jax.ShapeDtypeStruct((tokens, width), f32),
        grid=(tokens // tile,),
        in_specs=[
            pl.BlockSpec((tile, width), lambda i: (i, 0)),
            pl.BlockSpec((tile, exp_dev), lambda i: (i, 0)),
            pl.BlockSpec(expert_gate_up.shape, lambda i: (0, 0, 0, 0)),
            pl.BlockSpec(expert_down.shape, lambda i: (0, 0, 0)),
        ],
        out_specs=pl.BlockSpec((tile, width), lambda i: (i, 0)),
        compiler_params=params(),
        name="experts",
    )(gathered, shares, expert_gate_up, expert_down)
    weighted = lax.psum_scatter(parts, ("seq", "exp"), scatter_dimension=0, tiled=True)
    shared_both = jnp.einsum("rd,zdf->zrf", normed, shared_gate_up, preferred_element_type=f32)
    shared_act = (silu(shared_both[0]) * shared_both[1]).astype(bf16)
    shared_branch = jnp.dot(shared_act, shared_down, preferred_element_type=f32)
    shared_scale = jax.nn.sigmoid(jnp.dot(normed.astype(f32), shared_gate, precision=exact))
    moe_sum = weighted + shared_scale[:, None] * shared_branch
    return (hidden.astype(bf16), moe_sum.astype(bf16))


def solution(mesh):
    placed = (
        P("seq", None, "exp"),
        P("seq", "exp"),
        P("seq", "exp"),
        P(None, None, "exp"),
        P(None, "exp"),
        P("exp", "seq"),
        P("exp", "seq"),
        P(),
        P(),
        P("exp", None),
        P(("seq", "exp"), None),
        P(),
        P(("seq", "exp"), None),
        P(("seq", "exp"), None),
        P(("seq", "exp"), None, None, None),
        P(("seq", "exp"), None, None),
        P(),
        P(),
        P(),
    )
    return jax.shard_map(
        shards,
        mesh=mesh,
        in_specs=placed,
        out_specs=(P(("seq", "exp"), None), P(("seq", "exp"), None)),
        check_vma=False,
    )
```

time: 421 us -> 378 us (0.90)
  other arithmetic: 96.7 us -> 5.33 us
  waiting for transfers between devices: 163 us -> 213 us
  Pallas kernels: 0 us -> 42.2 us
  matrix products: 44.2 us -> 6.64 us
  local copies, waits for them, and re-layouts: 38.1 us -> 10 us
  blocking collectives: 53 us -> 70 us
    reduce_scatter x1 -> x2, waiting for transfers between devices: 50.1 us -> 211 us  [the longest x1 179 us: shards(): lax.psum_scatter(parts, ('seq', 'exp'), scatter_dimension=0, tiled=True)]
    another operation x5 -> x1, other arithmetic: 81.1 us -> 0.72 us  [shards(): cols = jnp.stack(cols, axis=1)]
    all_gather x2 -> x1, waiting for transfers between devices: 71 us -> 0.01 us  [shards(): gathered = lax.all_gather(normed, ('seq', 'exp'), axis=0, tiled=True)]
    all_gather x0 -> x1, blocking collectives: none -> 70 us  [shards(): shares = lax.all_gather(own_share, ('seq', 'exp'), axis=0, tiled=True)]
    all_to_all x1 -> x0, blocking collectives: 53 us -> none  [shards(): lax.all_to_all(send_four, ('seq', 'exp'), split_axis=0, concat_axis=0, ti...]
    pallas_call x0 -> x3, Pallas kernels: none -> 42.2 us  [the longest x1 20.8 us: shards(): pl.pallas_call(expert_kernel, out_shape=jax.ShapeDtypeStruct((tokens, wid...]
    all_to_all x1 -> x0, waiting for transfers between devices: 41.5 us -> none  [shards(): lax.all_to_all(experts_apply(lax.all_to_all(send_four, ('seq', 'exp'), sp...]
    dot_general x19 -> x3, matrix products: 39.5 us -> 3.61 us  [the longest x1 2.06 us: shards(): shared_branch = jnp.dot(shared_act, shared_down, preferred_element_type=f32)]
  transfers between devices with their start and end apart: 5 -> 6, of which waited for: 4 -> 4; matrix products, arithmetic and copies ran while one was open for 5% -> 3% of each run, Pallas kernels for 0% -> 0%
where the time goes in v1:
time: 378 us; the launch traced here: 371 us
  waiting for transfers between devices  213 us (56%)
  blocking collectives  70 us (19%)
  Pallas kernels  42.2 us (11%)
  between operations  13.9 us (4%)
  local copies, waits for them, and re-layouts  10 us (3%)
  starting transfers between devices  9.64 us (3%)
  matrix products  6.64 us (2%)
  other arithmetic  5.33 us (1%)
    reduce_scatter x1, waiting for transfers between devices, shards(): lax.psum_scatter(parts, ('seq', 'exp'), scatter_dimension=0, tiled=True)  179 us
    all_gather x1, blocking collectives, shards(): shares = lax.all_gather(own_share, ('seq', 'exp'), axis=0, tiled=True)  70 us
    reduce_scatter x1, waiting for transfers between devices, shards(): attn_part = lax.psum_scatter(part, 'exp', scatter_dimension=0, tiled=True)  32.3 us
    pallas_call x1, Pallas kernels, shards(): pl.pallas_call(expert_kernel, out_shape=jax.ShapeDtypeStruct((tokens, wid...  20.8 us
    pallas_call x1, Pallas kernels, shards(): pl.pallas_call(delta_kernel, out_shape=(jax.ShapeDtypeStruct((heads, leng...  16.8 us
    ppermute x3, starting transfers between devices, shifted(): return lax.ppermute(value, axis, pairs)  9.52 us
  transfers between devices with their start and end apart: 6, of which 4 were waited for; matrix products, arithmetic and copies ran while one was open for 3% of the time, Pallas kernels for 0%

profile of v1, /device:TPU:24, one launch (start us, length us, event | category | flops | bytes accessed | tf_op | source)
XLA Modules:
  0.0 371.0 jit_solution(5419158112185154580)
XLA Ops:
  7.2 0.0 copy-start
  7.2 0.0 reduce-scatter.3.cloned.1.call-start
  7.2 0.9 slice.32
  8.1 0.7 slice_bitcast_fusion.2
  8.8 1.7 collective-permute-start
  10.6 0.8 pad_dynamic-slice_fusion
  11.4 0.6 slice.37
  12.0 0.7 fusion.16
  12.7 0.6 convert_bitcast_fusion
  13.2 1.7 copy.32
  14.9 1.3 copy.34
  16.3 0.7 copy.31.cols_ref
  17.0 0.0 collective-permute-done.rim_ref
  17.0 0.0 copy-start.4
  17.0 0.6 copy-done.4
  17.7 16.8 %delta.1 = (f32[8,128,128]{2,1,0:T(8,128)}, bf16[8,128,128]{2,1,0:T(8,128)(2,1)}, bf16[8,128,128]{2,1,0:T(8,128)(2,1)}, f32[8,128,128]{2,1,0:T(8,128)}) custom-call(bf16[128,1024]{1,0:T(8,128)(2,1)} %bitcast.55, bf16[128,1024]{1,0:T(8,128)(2,1)} %v_ref.1, bf16[8,2048]{1,0:T(8,128)(2,1)} %copy-done.4, f32[4,1024]{1,0:T(4,128)} %bitcast.57, ...), custom_call_target="tpu_custom_call" | custom-call | tf_op jit(solution)/shard_map/delta/pallas_call | solution.py:186
  34.5 1.1 convert_element_type.32
  35.6 3.7 collective-permute-start.1
  39.3 1.1 collective-permute-done.1
  40.4 0.0 copy-start.2
  40.4 1.4 fusion.2
  41.8 0.0 copy-start.5
  41.8 4.1 %collective-permute-start.2 = (bf16[8,128,128]{2,1,0:T(8,128)(2,1)S(1)}, bf16[8,128,128]{2,1,0:T(8,128)(2,1)S(1)}, u32[]{:S(2)}, u32[]{:S(2)}) collective-permute-start(bf16[8,128,128]{2,1,0:T(8,128)(2,1)S(1)} %fusion.2), channel_id=1, source_target_pairs={{0,4},{4,8},{8,12},{12,16},{16,20},{20,24},{24,28},{1,5},{5,9},{9,... | collective-permute-start | bytes 786440 | tf_op jit(solution)/shard_map/ppermute | solution.py:33
  45.9 1.1 collective-permute-done.2.state_ref
  47.0 0.0 copy-start.3
  47.0 0.7 copy-done.3
  47.8 0.0 copy-start.6
  47.8 0.0 copy-start.7
  47.8 4.6 %project.1 = f32[128,2048]{1,0:T(8,128)} custom-call(bf16[8,128,128]{2,1,0:T(8,128)(2,1)} %get-tuple-element.6.query_ref, f32[8,128,128]{2,1,0:T(8,128)} %get-tuple-element.7.out_ref, bf16[8,128,128]{2,1,0:T(8,128)(2,1)} %copy-done.3, bf16[128,1024]{1,0:T(8,128)(2,1)} %z_ref.1, f32[1,128]{1,0:T(1,128)} %bitcast.60, bf16[1024,2048]{1,0:T(8,128)(2,1)} %weight_ref.1), custom_call_target="tpu_custom_call" | custom-call | tf_op jit(solution)/shard_map/project/pallas_call | solution.py:207
  52.4 0.0 reduce-scatter.3.cloned.1.call-update
  52.4 0.0 all-gather.2.cloned.1.call-start
  52.4 32.3 %reduce-scatter.3.cloned.1.call-done = f32[32,2048]{1,0:T(8,128)} async-done(((f32[128,2048]{1,0:T(8,128)}), f32[32,2048]{1,0:T(8,128)}) %reduce-scatter.3.cloned.1.call-update) | async-done | bytes 262160 | tf_op jit(solution)/shard_map/reduce_scatter | solution.py:215
  84.8 0.0 copy-done.2
  84.8 1.1 multiply_reduce_fusion
  85.9 0.0 copy-done.5
  85.9 1.7 multiply_convert_fusion
  87.6 0.0 all-gather.2.cloned.1.call-update
  87.6 0.0 reduce-scatter.5.cloned.1.call-start
  87.7 0.0 copy-done.6
  87.7 0.0 copy-done.7
  87.7 0.2 select_reduce_fusion
  87.8 70.0 %all_gather.7 = f32[1024,64]{1,0:T(8,128)S(1)} all-gather(f32[32,64]{1,0:T(8,128)S(1)} %select_reduce_fusion), channel_id=1, replica_groups=mesh['seq'=8,'exp'=4] {'seq','exp'}, dimensions={0}, use_global_device_ids=true | all-gather | bytes 270336 | tf_op jit(solution)/shard_map/all_gather | solution.py:171
  157.8 1.0 constant_dynamic-slice_fusion.share_ref
  158.9 0.0 all-gather.2.cloned.1.call-done.rows_ref
  158.9 20.8 %experts.1 = f32[1024,2048]{1,0:T(8,128)} custom-call(bf16[1024,2048]{1,0:T(8,128)(2,1)} %all-gather.2.cloned.1.call-done.rows_ref, f32[1024,2]{1,0:T(8,128)} %constant_dynamic-slice_fusion.share_ref, bf16[2,2,2048,512]{3,2,1,0:T(8,128)(2,1)} %up_ref.1, bf16[2,512,2048]{2,1,0:T(8,128)(2,1)} %down_ref.1), custom_call_target="tpu_custom_call" | custom-call | tf_op jit(solution)/shard_map/experts/pallas_call | solution.py:223
  179.6 0.0 copy-start.1
  179.6 0.0 copy-start.8
  179.6 0.0 reduce-scatter.5.cloned.1.call-update
  179.6 0.9 copy-done.1
  180.5 0.0 copy-done.8
  180.5 0.2 fusion.6
  180.7 3.0 convolution_bitcast_fusion
  183.7 178.7 %reduce-scatter.5.cloned.1.call-done = f32[32,2048]{1,0:T(8,128)} async-done(((f32[1024,2048]{1,0:T(8,128)}), f32[32,2048]{1,0:T(8,128)}) %reduce-scatter.5.cloned.1.call-update) | async-done | bytes 262160 | tf_op jit(solution)/shard_map/reduce_scatter | solution.py:237
  362.4 0.0 copy-done
  362.4 2.1 fusion.1
  (5 shorter events, 0.0 us)
Async XLA Ops:
  7.2 355.2 %copy-start = (bf16[512,2048]{1,0:T(8,128)(2,1)S(1)}, bf16[512,2048]{1,0:T(8,128)(2,1)}, u32[]{:S(2)}) copy-start(bf16[512,2048]{1,0:T(8,128)(2,1)} %param.36) | copy-start | bytes 6291460
  7.2 77.6 %reduce-scatter.3.cloned.1.call-start = ((), (), s32[]{:S(2)}) async-start(), calls=%async_computation.2 | async-start | bytes 1310720 | tf_op jit(solution)/shard_map/reduce_scatter | solution.py:215
  8.8 8.2 %collective-permute-start = (bf16[8,2048]{1,0:T(8,128)(2,1)S(1)}, bf16[8,2048]{1,0:T(8,128)(2,1)S(1)}, u32[]{:S(2)}, u32[]{:S(2)}) collective-permute-start(bf16[8,2048]{1,0:T(8,128)(2,1)S(1)} %pad_maximum_fusion), channel_id=1, source_target_pairs={{0,4},{4,8},{8,12},{12,16},{16,20},{20,24},{24,28},{1,5},{5,9},{9,... | collective-permute-start | bytes 98312 | tf_op jit(solution)/shard_map/ppermute | solution.py:33
  17.0 0.6 copy-start.4
  35.6 4.8 %collective-permute-start.1 = (bf16[8,128,128]{2,1,0:T(8,128)(2,1)S(1)}, bf16[8,128,128]{2,1,0:T(8,128)(2,1)S(1)}, u32[]{:S(2)}, u32[]{:S(2)}) collective-permute-start(bf16[8,128,128]{2,1,0:T(8,128)(2,1)S(1)} %convert_element_type.32), channel_id=1, source_target_pairs={{0,4},{4,8},{8,12},{12,16},{16,20},{20,24},{24,28},{1,5},{5,9},{9,... | collective-permute-start | bytes 786440 | tf_op jit(solution)/shard_map/ppermute | solution.py:33
  40.4 44.4 %copy-start.2 = (bf16[32,2048]{1,0:T(8,128)(2,1)S(1)}, bf16[32,2048]{1,0:T(8,128)(2,1)}, u32[]{:S(2)}) copy-start(bf16[32,2048]{1,0:T(8,128)(2,1)} %param.29) | copy-start | bytes 393220
  41.8 44.1 %copy-start.5 = (f32[2048]{0:T(1024)S(1)}, f32[2048]{0:T(1024)}, u32[]{:S(2)}) copy-start(f32[2048]{0:T(1024)} %param.30) | copy-start | bytes 24580
  41.8 5.2 %collective-permute-start.2 = (bf16[8,128,128]{2,1,0:T(8,128)(2,1)S(1)}, bf16[8,128,128]{2,1,0:T(8,128)(2,1)S(1)}, u32[]{:S(2)}, u32[]{:S(2)}) collective-permute-start(bf16[8,128,128]{2,1,0:T(8,128)(2,1)S(1)} %fusion.2), channel_id=1, source_target_pairs={{0,4},{4,8},{8,12},{12,16},{16,20},{20,24},{24,28},{1,5},{5,9},{9,... | collective-permute-start | bytes 786440 | tf_op jit(solution)/shard_map/ppermute | solution.py:33
  47.0 0.7 copy-start.3
  47.8 39.9 %copy-start.6 = (f32[32,10]{0,1:T(8,128)S(1)}, f32[32,10]{0,1:T(8,128)}, u32[]{:S(2)}) copy-start(f32[32,10]{0,1:T(8,128)} %param.32) | copy-start | bytes 3844
  47.8 39.9 %copy-start.7 = (s32[32,10]{0,1:T(8,128)S(1)}, s32[32,10]{0,1:T(8,128)}, u32[]{:S(2)}) copy-start(s32[32,10]{0,1:T(8,128)} %param.31) | copy-start | bytes 3844
  52.4 106.5 %all-gather.2.cloned.1.call-start = ((), (), s32[]{:S(2)}) async-start(), calls=%async_computation.3 | async-start | bytes 4325376 | tf_op jit(solution)/shard_map/all_gather | solution.py:220
  87.6 274.8 %reduce-scatter.5.cloned.1.call-start = ((), (), s32[]{:S(2)}) async-start(), calls=%async_computation.4 | async-start | bytes 8650752 | tf_op jit(solution)/shard_map/reduce_scatter | solution.py:237
  179.6 0.9 copy-start.1
  179.6 0.9 copy-start.8
Sparse Core Ops, SparseCore 0:
  52.5 32.1 reduce-scatter.2
  88.8 62.4 all-gather.1
  179.8 182.5 reduce-scatter.4

commit v2 on v1

--- a/solution.py
+++ b/solution.py
@@ -141,6 +141,287 @@
     return pltpu.CompilerParams(vmem_limit_bytes=56 * 1024 * 1024, **more)
 
 
+MESH = pl.DeviceIdType.MESH
+
+
+def moe_kernel(
+    query_ref, local_ref, state_ref, z_ref, head_gain_ref, residual_ref, post_gain_ref, share_ref,
+    gate_ref, weight_hbm, up_hbm, down_hbm, shared_up_hbm, shared_down_hbm,
+    hidden_ref, moe_ref,
+    weight, up, down, shared_up, shared_down, part, part_send, part_recv, tok, mine, core_send,
+    core_recv, pass_x, pass_y, send_x, send_y, recv_x, recv_y, back_send, back_recv,
+    load_sem, part_sems, tok_sems, core_sems, plane_sems, back_sems,
+):
+    heads, length, dim = local_ref.shape
+    rows, width = residual_ref.shape
+    depth = length // rows
+    seq = lax.axis_index("seq")
+    z = lax.axis_index("exp")
+    core = lax.rem(seq, 2)
+    x = lax.rem(seq // 2, 2)
+    y = seq // 4
+    to_core = (seq + 1 - 2 * core, z)
+    to_x = (seq + 2 - 4 * x, z)
+    to_y = (seq + 4 - 8 * y, z)
+    ahead = [(seq, lax.rem(z + k, depth)) for k in range(depth)]
+
+    loads = []
+    for n, (src, dst) in enumerate(
+        ((weight_hbm, weight), (shared_up_hbm, shared_up), (shared_down_hbm, shared_down),
+         (up_hbm, up), (down_hbm, down))
+    ):
+        load = pltpu.make_async_copy(src, dst, load_sem.at[n])
+        load.start()
+        loads.append(load)
+
+    barrier = pltpu.get_barrier_semaphore()
+    peers = [to_core, to_x, to_y] + ahead[1:]
+    for peer in peers:
+        pl.semaphore_signal(barrier, inc=1, device_id=peer, device_id_type=MESH)
+    pl.semaphore_wait(barrier, len(peers))
+
+    def send(src, dst, sems, at, peer):
+        copy = pltpu.make_async_remote_copy(
+            src_ref=src, dst_ref=dst, send_sem=sems.at[0, at], recv_sem=sems.at[1, at],
+            device_id=peer, device_id_type=MESH,
+        )
+        copy.start()
+        return copy
+
+    gated = []
+    for h in range(heads):
+        attn = local_ref[h] + dot(query_ref[h], state_ref[h])
+        scale = lax.rsqrt(jnp.mean(attn * attn, axis=1, keepdims=True) + 1e-06)
+        gate_z = z_ref[:, h * dim : (h + 1) * dim].astype(f32)
+        gated.append((attn * scale * head_gain_ref[...] * silu(gate_z)).astype(bf16))
+    gated = jnp.concatenate(gated, axis=1)
+    loads[0].wait()
+    tile = width // 4
+    for n in range(0, width, tile):
+        product = dot(gated, weight[:, n : n + tile])
+        part[:, n : n + tile] = product
+        part_send[:, n : n + tile] = product.astype(bf16)
+
+    def block_rows(k):
+        return pl.ds(pl.multiple_of(lax.rem(z + k, depth) * rows, rows), rows)
+
+    part_copies = {}
+    for k in range(depth - 1, 0, -1):
+        back = depth - k
+        part_copies[k] = send(
+            part_send.at[block_rows(k)], part_recv.at[back], part_sems, back, ahead[k]
+        )
+    hidden = residual_ref[...].astype(f32) + part[block_rows(0), :]
+    for k in range(1, depth):
+        part_copies[k].wait()
+    for k in range(1, depth):
+        hidden = hidden + part_recv[k].astype(f32)
+    hidden_ref[...] = hidden.astype(bf16)
+    normed = (
+        hidden * lax.rsqrt(jnp.mean(hidden * hidden, axis=1, keepdims=True) + 1e-06)
+        * post_gain_ref[...]
+    ).astype(bf16)
+    tok[0, :, 0:width] = normed
+    tok[0, :, width:] = share_ref[...]
+
+    def slot(group, other, k):
+        return (group * 2 + other) * depth + k
+
+    copies = []
+
+    def pass_on(at, to, peer):
+        copies.append(send(tok.at[at], tok.at[to], tok_sems, to, peer))
+
+    def arrived(at):
+        pltpu.make_async_remote_copy(
+            src_ref=tok.at[at], dst_ref=tok.at[at], send_sem=tok_sems.at[0, at],
+            recv_sem=tok_sems.at[1, at], device_id=to_core, device_id_type=MESH,
+        ).wait_recv()
+
+    def spread_own(k):
+        pass_on(slot(0, 0, k), slot(1, 0, k), to_x)
+        pass_on(slot(0, 0, k), slot(2, 0, k), to_y)
+        pass_on(slot(0, 0, k), slot(0, 1, k), to_core)
+
+    for k in range(1, depth):
+        pass_on(0, slot(0, 0, depth - k), ahead[k])
+    spread_own(0)
+    score = jax.nn.sigmoid(
+        jnp.sum(normed.astype(f32) * gate_ref[...], axis=1, keepdims=True)
+    )
+    loads[1].wait()
+    shared_gate = dot(normed, shared_up[0])
+    arrived(slot(0, 0, 1))
+    spread_own(1)
+    shared_act = (silu(shared_gate) * dot(normed, shared_up[1])).astype(bf16)
+    arrived(slot(0, 0, depth - 1))
+    spread_own(depth - 1)
+    loads[2].wait()
+    moe = score * dot(shared_act, shared_down[...])
+    for k in range(2, depth - 1):
+        arrived(slot(0, 0, k))
+        spread_own(k)
+    loads[3].wait()
+    loads[4].wait()
+
+    experts = up.shape[0]
+    lanes = tok.shape[2] - width
+    first = (seq * depth + z) * experts
+    lane = lax.broadcasted_iota(jnp.int32, (1, lanes), 1)
+    lane = lax.rem(lane, lanes // 2)
+    half = depth * rows
+    core_copies = {}
+
+    def work(group):
+        at = slot(group, 0, 0)
+        both = 2 * depth
+        held = tok[at : at + both, :, 0:width].reshape(both * rows, width)
+        shares = tok[at : at + both, :, width:].reshape(both * rows, lanes).astype(f32)
+        acts = []
+        for e in range(experts):
+            gate = dot(held, up[e, 0])
+            acts.append((silu(gate) * dot(held, up[e, 1])).astype(bf16))
+        share = [
+            jnp.sum(jnp.where(lane == first + e, shares, 0.0), axis=1, keepdims=True)
+            for e in range(experts)
+        ]
+        for n in range(0, width, tile):
+            total = share[0] * dot(acts[0], down[0, :, n : n + tile])
+            for e in range(1, experts):
+                total = total + share[e] * dot(acts[e], down[e, :, n : n + tile])
+            mine[group, :, n : n + tile] = total[:half]
+            core_send[group, :, n : n + tile] = total[half:]
+        core_copies[group] = send(
+            core_send.at[group], core_recv.at[group], core_sems, group, to_core
+        )
+
+    for k in range(depth):
+        arrived(slot(0, 1, k))
+    work(0)
+    middle = depth // 2
+    for k in range(depth):
+        arrived(slot(1, 0, k))
+        pass_on(slot(1, 0, k), slot(1, 1, k), to_core)
+        if k < middle:
+            pass_on(slot(1, 0, k), slot(3, 0, k), to_y)
+        arrived(slot(2, 0, k))
+        pass_on(slot(2, 0, k), slot(2, 1, k), to_core)
+        if k >= middle:
+            pass_on(slot(2, 0, k), slot(3, 0, k), to_x)
+    for k in range(depth):
+        arrived(slot(1, 1, k))
+    work(1)
+    for k in range(depth):
+        arrived(slot(3, 0, k))
+        pass_on(slot(3, 0, k), slot(3, 1, k), to_core)
+    for k in range(depth):
+        arrived(slot(2, 1, k))
+    work(2)
+    cut = middle * rows
+    low, high = slice(0, cut), slice(cut, half)
+    core_copies[1].wait()
+    send_x[0] = (mine[1, low, :] + core_recv[1, low, :]).astype(bf16)
+    plane = [send(send_x.at[0], recv_x.at[0], plane_sems, 0, to_x)]
+    core_copies[2].wait()
+    send_y[1] = (mine[2, high, :] + core_recv[2, high, :]).astype(bf16)
+    plane.append(send(send_y.at[1], recv_y.at[1], plane_sems, 1, to_y))
+    for k in range(depth):
+        arrived(slot(3, 1, k))
+    work(3)
+    core_copies[3].wait()
+    send_x[2] = (mine[3, low, :] + core_recv[3, low, :]).astype(bf16)
+    by_x = send(send_x.at[2], pass_x, plane_sems, 2, to_x)
+    send_y[2] = (mine[3, high, :] + core_recv[3, high, :]).astype(bf16)
+    by_y = send(send_y.at[2], pass_y, plane_sems, 3, to_y)
+    core_copies[0].wait()
+    own = mine[0] + core_recv[0]
+    mine[0] = own
+    by_x.wait()
+    send_y[0] = (mine[2, low, :] + core_recv[2, low, :] + pass_x[...].astype(f32)).astype(bf16)
+    plane.append(send(send_y.at[0], recv_y.at[0], plane_sems, 4, to_y))
+    by_y.wait()
+    send_x[1] = (mine[1, high, :] + core_recv[1, high, :] + pass_y[...].astype(f32)).astype(bf16)
+    plane.append(send(send_x.at[1], recv_x.at[1], plane_sems, 5, to_x))
+    for copy in plane:
+        copy.wait()
+    back_copies = []
+
+    def summed(k):
+        part_at, at = k // middle, k % middle * rows
+        return (
+            mine[0, k * rows : (k + 1) * rows, :]
+            + recv_x[part_at, at : at + rows, :].astype(f32)
+            + recv_y[part_at, at : at + rows, :].astype(f32)
+        )
+
+    for k in range(1, depth):
+        back_send[k] = summed(k).astype(bf16)
+        back_copies.append(
+            send(back_send.at[k], back_recv.at[depth - k], back_sems, depth - k, ahead[k])
+        )
+    moe = moe + summed(0)
+    for copy in back_copies:
+        copy.wait()
+    for k in range(1, depth):
+        moe = moe + back_recv[k].astype(f32)
+    moe_ref[...] = moe.astype(bf16)
+    for copy in copies:
+        copy.wait_send()
+
+
+def moe_call(
+    query, out_local, start, z_proj, head_gain, residual, post_gain, share, shared_gate,
+    out_weight, expert_gate_up, expert_down, shared_gate_up, shared_down,
+):
+    heads, length, dim = out_local.shape
+    rows, width = residual.shape
+    depth = length // rows
+    half, cut = depth * rows, depth // 2 * rows
+    row_block = jax.ShapeDtypeStruct((rows, width), bf16)
+    anywhere = pl.BlockSpec(memory_space=pl.ANY)
+    dma = pltpu.SemaphoreType.DMA
+    return pl.pallas_call(
+        moe_kernel,
+        out_shape=(row_block, row_block),
+        in_specs=[VM] * 9 + [anywhere] * 5,
+        out_specs=(VM, VM),
+        scratch_shapes=[
+            pltpu.VMEM(out_weight.shape, bf16),
+            pltpu.VMEM(expert_gate_up.shape, bf16),
+            pltpu.VMEM(expert_down.shape, bf16),
+            pltpu.VMEM(shared_gate_up.shape, bf16),
+            pltpu.VMEM(shared_down.shape, bf16),
+            pltpu.VMEM((length, width), f32),
+            pltpu.VMEM((length, width), bf16),
+            pltpu.VMEM((depth, rows, width), bf16),
+            pltpu.VMEM((8 * depth, rows, width + share.shape[1]), bf16),
+            pltpu.VMEM((4, half, width), f32),
+            pltpu.VMEM((4, half, width), f32),
+            pltpu.VMEM((4, half, width), f32),
+            pltpu.VMEM((cut, width), bf16),
+            pltpu.VMEM((cut, width), bf16),
+            pltpu.VMEM((3, cut, width), bf16),
+            pltpu.VMEM((3, cut, width), bf16),
+            pltpu.VMEM((2, cut, width), bf16),
+            pltpu.VMEM((2, cut, width), bf16),
+            pltpu.VMEM((depth, rows, width), bf16),
+            pltpu.VMEM((depth, rows, width), bf16),
+            dma((5,)),
+            dma((2, depth)),
+            dma((2, 8 * depth)),
+            dma((2, 4)),
+            dma((2, 6)),
+            dma((2, depth)),
+        ],
+        compiler_params=params(collective_id=1, has_side_effects=True),
+        name="moe",
+    )(
+        query, out_local, start, z_proj, head_gain.reshape(1, dim), residual,
+        post_gain.reshape(1, width), share, shared_gate.reshape(1, width), out_weight,
+        expert_gate_up, expert_down, shared_gate_up, shared_down,
+    )
+
+
 VM = pl.BlockSpec(memory_space=pltpu.VMEM)
 
 
@@ -168,9 +449,6 @@
         ),
         axis=1,
     )
-    shares = lax.all_gather(own_share, ("seq", "exp"), axis=0, tiled=True)
-    shares = lax.dynamic_slice_in_dim(shares, me * exp_dev, exp_dev, axis=1)
-
     flat_qk = qk_proj.reshape(length, 2 * key_cols)
     rim = shifted(
         jnp.concatenate([flat_qk[length - RIM :], v_proj[length - RIM :]], axis=1), "seq", 1
@@ -204,6 +482,16 @@
         before = shifted(state.astype(bf16), "seq", 1)
         state = add + jnp.einsum("hkl,hlv->hkv", move, before, preferred_element_type=f32)
     start = shifted(state.astype(bf16), "seq", 1)
+    if seq_count == 8 and lax.axis_size("exp") == 4 and 2 * own_share.shape[1] == 128:
+        rounded = own_share.astype(bf16)
+        rest = (own_share - rounded.astype(f32)).astype(bf16)
+        share = jnp.concatenate([rounded, rest], axis=1)
+        return moe_call(
+            query, out_local, start, z_proj, head_gain, residual, post_gain, share, shared_gate,
+            out_weight, expert_gate_up, expert_down, shared_gate_up, shared_down,
+        )
+    shares = lax.all_gather(own_share, ("seq", "exp"), axis=0, tiled=True)
+    shares = lax.dynamic_slice_in_dim(shares, me * exp_dev, exp_dev, axis=1)
     part = pl.pallas_call(
         project_kernel,
         out_shape=jax.ShapeDtypeStruct((length, width), f32),

time: 378 us -> 138 us (0.37); the launches traced: 371 us -> 137 us
  waiting for transfers between devices: 213 us -> 0.51 us
  blocking collectives: 70 us -> 0 us
  Pallas kernels: 42.2 us -> 110 us
  between operations: 13.9 us -> 0.72 us
  matrix products: 6.64 us -> 1.35 us
    reduce_scatter x2 -> x0, waiting for transfers between devices: 211 us -> none  [the longest x1 179 us: shards(): lax.psum_scatter(parts, ('seq', 'exp'), scatter_dimension=0, tiled=True)]
    all_gather x1 -> x0, blocking collectives: 70 us -> none  [shards(): shares = lax.all_gather(own_share, ('seq', 'exp'), axis=0, tiled=True)]
    pallas_call x2 -> x1, Pallas kernels: 25.3 us -> 92.9 us  [moe_call(): pl.pallas_call(moe_kernel, out_shape=(row_block, row_block), in_specs=[VM...]
    dot_general x3 -> x0, matrix products: 5.25 us -> none  [the longest x1 3.03 us: shards(): jnp.einsum('rd,zdf->zrf', normed, shared_gate_up, preferred_element_type=...]
    unnamed x22 -> x10, local copies, waits for them, and re-layouts: 5.99 us -> 8.18 us
  transfers between devices with their start and end apart: 6 -> 3, of which waited for: 4 -> 2; matrix products, arithmetic and copies ran while one was open for 3% -> 6% of each run, Pallas kernels for 0% -> 0%
where the time goes in v2:
time: 138 us; the launch traced here: 137 us
  Pallas kernels  110 us (80%)
  local copies, waits for them, and re-layouts  11 us (8%)
  starting transfers between devices  9.7 us (7%)
  other arithmetic  4 us (3%)
    pallas_call x1, Pallas kernels, moe_call(): pl.pallas_call(moe_kernel, out_shape=(row_block, row_block), in_specs=[VM...  92.9 us
    pallas_call x1, Pallas kernels, shards(): pl.pallas_call(delta_kernel, out_shape=(jax.ShapeDtypeStruct((heads, leng...  16.9 us
    ppermute x3, starting transfers between devices, shifted(): return lax.ppermute(value, axis, pairs)  9.7 us
    unnamed x10, local copies, waits for them, and re-layouts  8.18 us
  transfers between devices with their start and end apart: 3, of which 2 were waited for; matrix products, arithmetic and copies ran while one was open for 6% of the time, Pallas kernels for 0%

profile of v2, /device:TPU:24, one launch (start us, length us, event | category | flops | bytes accessed | tf_op | source)
XLA Modules:
  0.0 137.1 jit_solution(12011146741521470225)
XLA Ops:
  0.6 0.7 slice.26
  1.4 0.7 slice_bitcast_fusion
  2.1 1.7 %collective-permute-start = (bf16[8,2048]{1,0:T(8,128)(2,1)S(1)}, bf16[8,2048]{1,0:T(8,128)(2,1)S(1)}, u32[]{:S(2)}, u32[]{:S(2)}) collective-permute-start(bf16[8,2048]{1,0:T(8,128)(2,1)S(1)} %pad_maximum_fusion), channel_id=1, source_target_pairs={{0,4},{4,8},{8,12},{12,16},{16,20},{20,24},{24,28},{1,5},{5,9},{9,... | collective-permute-start | bytes 98312 | tf_op jit(solution)/shard_map/ppermute | solution.py:33
  3.9 0.8 pad_dynamic-slice_fusion
  4.6 0.6 slice.31
  5.2 0.7 fusion.4
  5.9 0.6 convert_bitcast_fusion
  6.6 1.7 %copy.32 = bf16[16,8,2,512]{3,1,2,0:T(8,128)(2,1)} copy(bf16[16,8,2,512]{3,2,1,0:T(2,128)(2,1)} %bitcast.26) | data formatting | bytes 524288
  8.3 1.3 copy.34
  9.6 0.7 copy.31.cols_ref
  10.3 0.0 collective-permute-done.rim_ref
  10.4 0.0 copy-start.1
  10.4 0.6 copy-done.1
  11.0 16.9 %delta.1 = (f32[8,128,128]{2,1,0:T(8,128)}, bf16[8,128,128]{2,1,0:T(8,128)(2,1)}, bf16[8,128,128]{2,1,0:T(8,128)(2,1)}, f32[8,128,128]{2,1,0:T(8,128)}) custom-call(bf16[128,1024]{1,0:T(8,128)(2,1)} %bitcast.25, bf16[128,1024]{1,0:T(8,128)(2,1)} %v_ref.1, bf16[8,2048]{1,0:T(8,128)(2,1)} %copy-done.1, f32[4,1024]{1,0:T(4,128)} %bitcast.27, ...), custom_call_target="tpu_custom_call" | custom-call | tf_op jit(solution)/shard_map/delta/pallas_call | solution.py:464
  27.9 1.1 convert_element_type.24
  28.9 3.7 %collective-permute-start.1 = (bf16[8,128,128]{2,1,0:T(8,128)(2,1)S(1)}, bf16[8,128,128]{2,1,0:T(8,128)(2,1)S(1)}, u32[]{:S(2)}, u32[]{:S(2)}) collective-permute-start(bf16[8,128,128]{2,1,0:T(8,128)(2,1)S(1)} %convert_element_type.24), channel_id=1, source_target_pairs={{0,4},{4,8},{8,12},{12,16},{16,20},{20,24},{24,28},{1,5},{5,9},{9,... | collective-permute-start | bytes 786440 | tf_op jit(solution)/shard_map/ppermute | solution.py:33
  32.6 0.9 select_reduce_fusion
  33.5 0.3 collective-permute-done.1
  33.8 1.4 fusion
  35.1 4.3 %collective-permute-start.2 = (bf16[8,128,128]{2,1,0:T(8,128)(2,1)S(1)}, bf16[8,128,128]{2,1,0:T(8,128)(2,1)S(1)}, u32[]{:S(2)}, u32[]{:S(2)}) collective-permute-start(bf16[8,128,128]{2,1,0:T(8,128)(2,1)S(1)} %fusion), channel_id=1, source_target_pairs={{0,4},{4,8},{8,12},{12,16},{16,20},{20,24},{24,28},{1,5},{5,9},{9,... | collective-permute-start | bytes 786440 | tf_op jit(solution)/shard_map/ppermute | solution.py:33
  39.4 0.7 pad_maximum_fusion.1.share_ref
  40.1 0.3 collective-permute-done.2.state_ref
  40.4 0.0 copy-start
  40.4 0.7 copy-done
  41.1 92.9 %moe.1 = (bf16[32,2048]{1,0:T(8,128)(2,1)}, bf16[32,2048]{1,0:T(8,128)(2,1)}) custom-call(bf16[8,128,128]{2,1,0:T(8,128)(2,1)} %get-tuple-element.6.query_ref, f32[8,128,128]{2,1,0:T(8,128)} %get-tuple-element.7.local_ref, bf16[8,128,128]{2,1,0:T(8,128)(2,1)} %copy-done, bf16[128,1024]{1,0:T(8,128)(2,1)} %z_ref.1, f32[1,128]{1,0:T(1,128)} %bitcast.32, ...), custom_call_target="tpu_custom_call" | custom-call | tf_op jit(solution)/shard_map/moe/pallas_call | solution.py:383
  134.0 1.6 %copy.37 = bf16[32,2048]{1,0:T(8,128)(2,1)} copy(bf16[32,2048]{1,0:T(8,128)(2,1)} %get-tuple-element.20) | data formatting | bytes 262144
  135.5 1.6 %copy.38 = bf16[32,2048]{1,0:T(8,128)(2,1)} copy(bf16[32,2048]{1,0:T(8,128)(2,1)} %get-tuple-element.21) | data formatting | bytes 262144
  (5 shorter events, 0.0 us)
Async XLA Ops:
  2.1 8.2 %collective-permute-start = (bf16[8,2048]{1,0:T(8,128)(2,1)S(1)}, bf16[8,2048]{1,0:T(8,128)(2,1)S(1)}, u32[]{:S(2)}, u32[]{:S(2)}) collective-permute-start(bf16[8,2048]{1,0:T(8,128)(2,1)S(1)} %pad_maximum_fusion), channel_id=1, source_target_pairs={{0,4},{4,8},{8,12},{12,16},{16,20},{20,24},{24,28},{1,5},{5,9},{9,... | collective-permute-start | bytes 98312 | tf_op jit(solution)/shard_map/ppermute | solution.py:33
  10.4 0.6 copy-start.1
  28.9 4.8 %collective-permute-start.1 = (bf16[8,128,128]{2,1,0:T(8,128)(2,1)S(1)}, bf16[8,128,128]{2,1,0:T(8,128)(2,1)S(1)}, u32[]{:S(2)}, u32[]{:S(2)}) collective-permute-start(bf16[8,128,128]{2,1,0:T(8,128)(2,1)S(1)} %convert_element_type.24), channel_id=1, source_target_pairs={{0,4},{4,8},{8,12},{12,16},{16,20},{20,24},{24,28},{1,5},{5,9},{9,... | collective-permute-start | bytes 786440 | tf_op jit(solution)/shard_map/ppermute | solution.py:33
  35.1 5.2 %collective-permute-start.2 = (bf16[8,128,128]{2,1,0:T(8,128)(2,1)S(1)}, bf16[8,128,128]{2,1,0:T(8,128)(2,1)S(1)}, u32[]{:S(2)}, u32[]{:S(2)}) collective-permute-start(bf16[8,128,128]{2,1,0:T(8,128)(2,1)S(1)} %fusion), channel_id=1, source_target_pairs={{0,4},{4,8},{8,12},{12,16},{16,20},{20,24},{24,28},{1,5},{5,9},{9,... | collective-permute-start | bytes 786440 | tf_op jit(solution)/shard_map/ppermute | solution.py:33
  40.4 0.7 copy-start

commit v3 on v2

--- a/solution.py
+++ b/solution.py
@@ -10,7 +10,7 @@
 exact = lax.Precision.HIGHEST
 f32 = jnp.float32
 bf16 = jnp.bfloat16
-RIM = 8
+RIM = 16
 
 
 def dot(a, b, dims=((1,), (0,))):
@@ -33,86 +33,114 @@
     return lax.ppermute(value, axis, pairs)
 
 
-def unit_lower_inverse(lower, row, col):
-    size = lower.shape[0]
-    inverse = jnp.where(row == col, 1.0, jnp.where(row // 2 == col // 2, -lower, 0.0))
+def dot_split(a, b, dims=((1,), (0,))):
+    a_low = a - a.astype(bf16).astype(f32)
+    b_low = b - b.astype(bf16).astype(f32)
+    return dot(a, b, dims) + (dot(a_low, b, dims) + dot(a, b_low, dims))
+
+
+def unit_lower_inverses(lowers, row, col):
+    size = lowers[0].shape[0]
+    inverses = [
+        jnp.where(row == col, 1.0, jnp.where(row // 2 == col // 2, -lower, 0.0))
+        for lower in lowers
+    ]
     span = 2
     while span < size:
         joins = (row // (2 * span) == col // (2 * span)) & (row // span != col // span)
-        corner = jnp.where(joins, lower, 0.0)
-        inverse = inverse - dot(dot(inverse, corner), inverse)
+        corners = [
+            dot(inverse, jnp.where(joins, lower, 0.0))
+            for inverse, lower in zip(inverses, lowers)
+        ]
+        inverses = [
+            inverse - dot(corner, inverse) for inverse, corner in zip(inverses, corners)
+        ]
         span *= 2
-    return inverse
+    return inverses
 
 
 def conv_silu(prev, own, taps, masks):
     length = own.shape[0]
     ext = jnp.concatenate([prev, own], axis=0).astype(f32)
-    kernel_len = taps.shape[0]
-    total = taps[kernel_len - 1 : kernel_len] * ext[RIM:]
-    for i in range(kernel_len - 1):
-        at = RIM - (kernel_len - 1) + i
-        total = total + taps[i : i + 1] * (ext[at : at + length] * masks[:, i : i + 1])
+    total = taps[-1] * ext[RIM:]
+    for i in range(len(taps) - 1):
+        at = RIM - (len(taps) - 1) + i
+        total = total + taps[i] * (ext[at : at + length] * masks[i])
     return silu(total)
+
+
+def delta_body(
+    conv_key, conv_value, decay, beta, doc_col, doc_row, enters, out_ref, query_ref, move_ref,
+    add_ref, after,
+):
+    length = doc_row.shape[1]
+    heads, _, dim = add_ref.shape
+    row = lax.broadcasted_iota(jnp.int32, (length, length), 0)
+    col = lax.broadcasted_iota(jnp.int32, (length, length), 1)
+    keep = (row >= col) & (doc_col == doc_row)
+    keep_f = keep.astype(f32)
+    strict = jnp.where(row > col, keep_f, 0.0)
+    eye = (row == col).astype(f32)
+    cum_row = dot_exact(decay, (row <= col).astype(f32))
+    cum_col = dot_exact((row >= col).astype(f32), decay, ((1,), (1,)))
+    beta_col = dot_exact(eye, beta, ((1,), (1,)))
+    ends = (doc_col == doc_col[length - 1 : length]).astype(f32)
+    batch = 4 if heads % 4 == 0 else 2
+    for first in range(0, heads, batch):
+        group = range(first, first + batch)
+        q, k, qk, kk = {}, {}, {}, {}
+        for j in range(first // 2, (first + batch) // 2):
+            qj, kj = conv_key(0, j), conv_key(1, j)
+            q[j] = qj * (lax.rsqrt(jnp.sum(qj * qj, axis=1, keepdims=True) + 1e-06) * dim ** (-0.5))
+            k[j] = kj * lax.rsqrt(jnp.sum(kj * kj, axis=1, keepdims=True) + 1e-06)
+            both = dot_exact(jnp.concatenate([q[j], k[j]], axis=0), k[j], ((1,), (1,)))
+            qk[j], kk[j] = both[:length], both[length:]
+        within, carried, lowers = [], [], []
+        for h in group:
+            spread = cum_col[:, h : h + 1] - cum_row[h : h + 1, :]
+            within.append(jnp.exp(jnp.where(keep, spread, 0.0)) * keep_f)
+            carried.append(jnp.exp(cum_col[:, h : h + 1]) * enters)
+            lowers.append(beta_col[:, h : h + 1] * within[-1] * kk[h // 2] * strict)
+        inverses = unit_lower_inverses(lowers, row, col)
+        solved = []
+        for n, h in enumerate(group):
+            b = beta_col[:, h : h + 1]
+            sides = jnp.concatenate([b * conv_value(h), (b * carried[n]) * k[h // 2]], axis=1)
+            solved.append(dot_split(inverses[n], sides))
+        for n, h in enumerate(group):
+            last = cum_col[length - 1 : length, h : h + 1]
+            to_end = jnp.exp((last - cum_col[:, h : h + 1]) * ends) * ends
+            end = dot(to_end * k[h // 2], solved[n], ((0,), (0,)))
+            add_ref[h] = end[:, :dim]
+            move_ref[h] = (carried[n][length - 1 : length] * eye - end[:, dim:]).astype(bf16)
+        after(first, batch)
+        for n, h in enumerate(group):
+            local = dot_split(qk[h // 2] * within[n], solved[n])
+            out_ref[h] = local[:, :dim]
+            query_ref[h] = (carried[n] * q[h // 2] - local[:, dim:]).astype(bf16)
 
 
 def delta_kernel(
     qk_ref, v_ref, rim_ref, taps_qk_ref, taps_v_ref, decay_ref, beta_ref, cols_ref, row_ref,
     out_ref, query_ref, move_ref, add_ref,
 ):
-    length = v_ref.shape[0]
-    heads = decay_ref.shape[0]
-    dim = v_ref.shape[1] // heads
+    dim = add_ref.shape[1]
     key_cols = taps_qk_ref.shape[1] // 2
-    row = lax.broadcasted_iota(jnp.int32, (length, length), 0)
-    col = lax.broadcasted_iota(jnp.int32, (length, length), 1)
-    masks = cols_ref[...]
-    doc_col = masks[:, 4:5]
-    enters = masks[:, 5:6]
-    doc_row = row_ref[0:1, :]
-    keep = (row >= col) & (doc_col == doc_row)
-    keep_f = keep.astype(f32)
-    strict = jnp.where(row > col, keep_f, 0.0)
-    decay = decay_ref[...]
-    cum_row = dot_exact(decay, (row <= col).astype(f32))
-    cum_col = dot_exact((row >= col).astype(f32), decay, ((1,), (1,)))
-    beta_col = dot_exact((row == col).astype(f32), beta_ref[...], ((1,), (1,)))
-    ends = (doc_col == doc_col[length - 1 : length]).astype(f32)
-    eye = (row == col).astype(f32)
-
-    def head_cols(ref, rim_at, taps_ref, at):
-        return conv_silu(
-            rim_ref[:, rim_at + at : rim_at + at + dim],
-            ref[:, at : at + dim],
-            taps_ref[:, at : at + dim],
-            masks,
-        )
-
-    for j in range(heads // 2):
-        q = head_cols(qk_ref, 0, taps_qk_ref, j * dim)
-        k = head_cols(qk_ref, 0, taps_qk_ref, key_cols + j * dim)
-        q = q * (lax.rsqrt(jnp.sum(q * q, axis=1, keepdims=True) + 1e-06) * dim ** (-0.5))
-        k = k * lax.rsqrt(jnp.sum(k * k, axis=1, keepdims=True) + 1e-06)
-        both = dot_exact(jnp.concatenate([q, k], axis=0), k, ((1,), (1,)))
-        qk, kk = both[:length], both[length:]
-        for h in (2 * j, 2 * j + 1):
-            v = head_cols(v_ref, 2 * key_cols, taps_v_ref, h * dim)
-            spread = cum_col[:, h : h + 1] - cum_row[h : h + 1, :]
-            within = jnp.exp(jnp.where(keep, spread, 0.0)) * keep_f
-            carried = jnp.exp(cum_col[:, h : h + 1]) * enters
-            beta = beta_col[:, h : h + 1]
-            inverse = unit_lower_inverse(beta * within * kk * strict, row, col)
-            solved = dot(
-                inverse, jnp.concatenate([beta * v, (beta * carried) * k], axis=1)
-            ).astype(bf16)
-            local = dot(qk * within, solved)
-            last = cum_col[length - 1 : length, h : h + 1]
-            to_end = jnp.exp((last - cum_col[:, h : h + 1]) * ends) * ends
-            end = dot(to_end * k, solved, ((0,), (0,)))
-            out_ref[h] = local[:, :dim]
-            query_ref[h] = (carried * q - local[:, dim:]).astype(bf16)
-            add_ref[h] = end[:, :dim]
-            move_ref[h] = (carried[length - 1 : length] * eye - end[:, dim:]).astype(bf16)
+    kernel_len = taps_v_ref.shape[0]
+    cols = cols_ref[...]
+    masks = [cols[:, i : i + 1] for i in range(kernel_len - 1)]
+
+    def head(ref, rim_at, taps_ref, at):
+        taps = [taps_ref[i : i + 1, at : at + dim] for i in range(kernel_len)]
+        rim = rim_ref[:, rim_at + at : rim_at + at + dim]
+        return conv_silu(rim, ref[:, at : at + dim], taps, masks)
+
+    delta_body(
+        lambda half, j: head(qk_ref, 0, taps_qk_ref, half * key_cols + j * dim),
+        lambda h: head(v_ref, 2 * key_cols, taps_v_ref, h * dim),
+        decay_ref[...], beta_ref[...], cols[:, 4:5], row_ref[0:1, :], cols[:, 5:6],
+        out_ref, query_ref, move_ref, add_ref, lambda first, batch: None,
+    )
 
 
 def project_kernel(query_ref, out_ref, state_ref, z_ref, gain_ref, weight_ref, part_ref):
@@ -145,21 +173,27 @@
 
 
 def moe_kernel(
-    query_ref, local_ref, state_ref, z_ref, head_gain_ref, residual_ref, post_gain_ref, share_ref,
-    gate_ref, weight_hbm, up_hbm, down_hbm, shared_up_hbm, shared_down_hbm,
+    qk_ref, v_ref, taps_qk_ref, taps_v_ref, decay_ref, beta_ref, doc_ref, ids_ref, route_ref,
+    z_ref, head_gain_ref, residual_ref, post_gain_ref, gate_ref, weight_hbm, up_hbm, down_hbm, shared_up_hbm, shared_down_hbm,
     hidden_ref, moe_ref,
+    rim_qk, rim_v, local_ref, query_ref, move, add, add_send, add_recv, state_send, state_recv,
     weight, up, down, shared_up, shared_down, part, part_send, part_recv, tok, mine, core_send,
     core_recv, pass_x, pass_y, send_x, send_y, recv_x, recv_y, back_send, back_recv,
-    load_sem, part_sems, tok_sems, core_sems, plane_sems, back_sems,
+    load_sem, rim_sems, hop_sems, part_sems, tok_sems, core_sems, plane_sems, back_sems,
 ):
     heads, length, dim = local_ref.shape
     rows, width = residual_ref.shape
     depth = length // rows
+    experts = up.shape[0]
+    lanes = tok.shape[2] - width
     seq = lax.axis_index("seq")
     z = lax.axis_index("exp")
     core = lax.rem(seq, 2)
     x = lax.rem(seq // 2, 2)
     y = seq // 4
+    seqs = lax.axis_size("seq")
+    to_next = (lax.rem(seq + 1, seqs), z)
+    to_last = (lax.rem(seq + seqs - 1, seqs), z)
     to_core = (seq + 1 - 2 * core, z)
     to_x = (seq + 2 - 4 * x, z)
     to_y = (seq + 4 - 8 * y, z)
@@ -175,7 +209,7 @@
         loads.append(load)
 
     barrier = pltpu.get_barrier_semaphore()
-    peers = [to_core, to_x, to_y] + ahead[1:]
+    peers = [to_next, to_last, to_core, to_x, to_y] + ahead[1:]
     for peer in peers:
         pl.semaphore_signal(barrier, inc=1, device_id=peer, device_id_type=MESH)
     pl.semaphore_wait(barrier, len(peers))
@@ -188,9 +222,70 @@
         copy.start()
         return copy
 
+    tail = pl.ds(length - RIM, RIM)
+    rims = [
+        send(qk_ref.at[tail], rim_qk, rim_sems, 0, to_next),
+        send(v_ref.at[tail], rim_v, rim_sems, 1, to_next),
+    ]
+    kernel_len = taps_v_ref.shape[0]
+    doc_row = doc_ref[:, pl.ds(pl.multiple_of(seq * length, length), length)].astype(f32)
+    before = jnp.maximum(seq - 1, 0)
+    doc_before = doc_ref[:, pl.ds(pl.multiple_of(before * length, length), length)].astype(f32)
+    doc_before = jnp.where(seq == 0, -1.0, doc_before)
+    doc_both = jnp.broadcast_to(
+        jnp.concatenate([doc_before, doc_row], axis=1), (8, 2 * length)
+    )
+    token = lax.broadcasted_iota(jnp.int32, (length, 2 * length), 0) + length
+    other = lax.broadcasted_iota(jnp.int32, (length, 2 * length), 1)
+    doc_cols = [
+        dot_exact((other == token - i).astype(f32), doc_both, ((1,), (1,)))[:, 0:1]
+        for i in range(kernel_len)
+    ]
+    enters = (doc_cols[0] == doc_before[:, length - 1 : length]).astype(f32)
+    same = [(doc_cols[i] == doc_cols[0]).astype(f32) for i in range(kernel_len - 1, 0, -1)]
+
+    def key_head(part_at, j):
+        at = slice(j * dim, (j + 1) * dim)
+        taps = [taps_qk_ref[i, part_at : part_at + 1, at] for i in range(kernel_len)]
+        at = slice((part_at * heads // 2 + j) * dim, (part_at * heads // 2 + j + 1) * dim)
+        return conv_silu(rim_qk[:, at], qk_ref[:, at], taps, same)
+
+    def value_head(h):
+        at = slice(h * dim, (h + 1) * dim)
+        taps = [taps_v_ref[i : i + 1, at] for i in range(kernel_len)]
+        return conv_silu(rim_v[:, at], v_ref[:, at], taps, same)
+
+    hops = []
+
+    def hop(first, batch):
+        group = pl.ds(first, batch)
+        add_send[group] = add[group].astype(bf16)
+        at = first // batch
+        copy = send(add_send.at[group], add_recv.at[group], hop_sems, at, to_next)
+        hops.append((first, batch, at, copy))
+
+    for copy in rims:
+        copy.wait()
+    delta_body(
+        key_head, value_head, decay_ref[...], beta_ref[...], doc_cols[0], doc_row, enters,
+        local_ref, query_ref, move, add, hop,
+    )
+    states = []
+    for first, batch, at, copy in hops:
+        copy.wait()
+        for h in range(first, first + batch):
+            state_send[h] = (add[h] + dot(move[h], add_recv[h])).astype(bf16)
+        group = pl.ds(first, batch)
+        states.append(
+            send(
+                state_send.at[group], state_recv.at[group], hop_sems, len(hops) + at, to_next
+            )
+        )
     gated = []
     for h in range(heads):
-        attn = local_ref[h] + dot(query_ref[h], state_ref[h])
+        if h % hops[0][1] == 0:
+            states[h // hops[0][1]].wait()
+        attn = local_ref[h] + dot(query_ref[h], state_recv[h])
         scale = lax.rsqrt(jnp.mean(attn * attn, axis=1, keepdims=True) + 1e-06)
         gate_z = z_ref[:, h * dim : (h + 1) * dim].astype(f32)
         gated.append((attn * scale * head_gain_ref[...] * silu(gate_z)).astype(bf16))
@@ -222,7 +317,13 @@
         * post_gain_ref[...]
     ).astype(bf16)
     tok[0, :, 0:width] = normed
-    tok[0, :, width:] = share_ref[...]
+    lane = lax.broadcasted_iota(jnp.int32, (1, lanes), 1)
+    named = lax.rem(lane, lanes // 2)
+    share = jnp.zeros((rows, lanes), f32)
+    for n in range(ids_ref.shape[1]):
+        share = share + jnp.where(ids_ref[:, n : n + 1] == named, route_ref[:, n : n + 1], 0.0)
+    rest = share - share.astype(bf16).astype(f32)
+    tok[0, :, width:] = jnp.where(lane < lanes // 2, share, rest).astype(bf16)
 
     def slot(group, other, k):
         return (group * 2 + other) * depth + k
@@ -246,29 +347,13 @@
     for k in range(1, depth):
         pass_on(0, slot(0, 0, depth - k), ahead[k])
     spread_own(0)
-    score = jax.nn.sigmoid(
-        jnp.sum(normed.astype(f32) * gate_ref[...], axis=1, keepdims=True)
-    )
-    loads[1].wait()
-    shared_gate = dot(normed, shared_up[0])
-    arrived(slot(0, 0, 1))
-    spread_own(1)
-    shared_act = (silu(shared_gate) * dot(normed, shared_up[1])).astype(bf16)
-    arrived(slot(0, 0, depth - 1))
-    spread_own(depth - 1)
-    loads[2].wait()
-    moe = score * dot(shared_act, shared_down[...])
-    for k in range(2, depth - 1):
+    for k in [1, depth - 1] + list(range(2, depth - 1)):
         arrived(slot(0, 0, k))
         spread_own(k)
     loads[3].wait()
     loads[4].wait()
 
-    experts = up.shape[0]
-    lanes = tok.shape[2] - width
     first = (seq * depth + z) * experts
-    lane = lax.broadcasted_iota(jnp.int32, (1, lanes), 1)
-    lane = lax.rem(lane, lanes // 2)
     half = depth * rows
     core_copies = {}
 
@@ -282,7 +367,7 @@
             gate = dot(held, up[e, 0])
             acts.append((silu(gate) * dot(held, up[e, 1])).astype(bf16))
         share = [
-            jnp.sum(jnp.where(lane == first + e, shares, 0.0), axis=1, keepdims=True)
+            jnp.sum(jnp.where(named == first + e, shares, 0.0), axis=1, keepdims=True)
             for e in range(experts)
         ]
         for n in range(0, width, tile):
@@ -295,9 +380,6 @@
             core_send.at[group], core_recv.at[group], core_sems, group, to_core
         )
 
-    for k in range(depth):
-        arrived(slot(0, 1, k))
-    work(0)
     middle = depth // 2
     for k in range(depth):
         arrived(slot(1, 0, k))
@@ -333,6 +415,9 @@
     by_x = send(send_x.at[2], pass_x, plane_sems, 2, to_x)
     send_y[2] = (mine[3, high, :] + core_recv[3, high, :]).astype(bf16)
     by_y = send(send_y.at[2], pass_y, plane_sems, 3, to_y)
+    for k in range(depth):
+        arrived(slot(0, 1, k))
+    work(0)
     core_copies[0].wait()
     own = mine[0] + core_recv[0]
     mine[0] = own
@@ -359,7 +444,14 @@
         back_copies.append(
             send(back_send.at[k], back_recv.at[depth - k], back_sems, depth - k, ahead[k])
         )
-    moe = moe + summed(0)
+    normed = tok[0, :, 0:width]
+    score = jax.nn.sigmoid(
+        jnp.sum(normed.astype(f32) * gate_ref[...], axis=1, keepdims=True)
+    )
+    loads[1].wait()
+    shared_act = (silu(dot(normed, shared_up[0])) * dot(normed, shared_up[1])).astype(bf16)
+    loads[2].wait()
+    moe = score * dot(shared_act, shared_down[...]) + summed(0)
     for copy in back_copies:
         copy.wait()
     for k in range(1, depth):
@@ -370,10 +462,13 @@
 
 
 def moe_call(
-    query, out_local, start, z_proj, head_gain, residual, post_gain, share, shared_gate,
-    out_weight, expert_gate_up, expert_down, shared_gate_up, shared_down,
+    flat_qk, v_proj, z_proj, conv_qk, conv_v, decay_log, beta_gate, doc_ids, head_gain,
+    out_weight, residual, post_gain, route_ids, route_weight, expert_gate_up, expert_down,
+    shared_gate_up, shared_down, shared_gate,
 ):
-    heads, length, dim = out_local.shape
+    heads, length = decay_log.shape
+    dim = v_proj.shape[1] // heads
+    lanes = 128
     rows, width = residual.shape
     depth = length // rows
     half, cut = depth * rows, depth // 2 * rows
@@ -383,9 +478,19 @@
     return pl.pallas_call(
         moe_kernel,
         out_shape=(row_block, row_block),
-        in_specs=[VM] * 9 + [anywhere] * 5,
+        in_specs=[VM] * 14 + [anywhere] * 5,
         out_specs=(VM, VM),
         scratch_shapes=[
+            pltpu.VMEM((RIM, flat_qk.shape[1]), bf16),
+            pltpu.VMEM((RIM, v_proj.shape[1]), bf16),
+            pltpu.VMEM((heads, length, dim), f32),
+            pltpu.VMEM((heads, length, dim), bf16),
+            pltpu.VMEM((heads, dim, dim), bf16),
+            pltpu.VMEM((heads, dim, dim), f32),
+            pltpu.VMEM((heads, dim, dim), bf16),
+            pltpu.VMEM((heads, dim, dim), bf16),
+            pltpu.VMEM((heads, dim, dim), bf16),
+            pltpu.VMEM((heads, dim, dim), bf16),
             pltpu.VMEM(out_weight.shape, bf16),
             pltpu.VMEM(expert_gate_up.shape, bf16),
             pltpu.VMEM(expert_down.shape, bf16),
@@ -394,7 +499,7 @@
             pltpu.VMEM((length, width), f32),
             pltpu.VMEM((length, width), bf16),
             pltpu.VMEM((depth, rows, width), bf16),
-            pltpu.VMEM((8 * depth, rows, width + share.shape[1]), bf16),
+            pltpu.VMEM((8 * depth, rows, width + lanes), bf16),
             pltpu.VMEM((4, half, width), f32),
             pltpu.VMEM((4, half, width), f32),
             pltpu.VMEM((4, half, width), f32),
@@ -407,6 +512,8 @@
             pltpu.VMEM((depth, rows, width), bf16),
             pltpu.VMEM((depth, rows, width), bf16),
             dma((5,)),
+            dma((2, 2)),
+            dma((2, heads)),
             dma((2, depth)),
             dma((2, 8 * depth)),
             dma((2, 4)),
@@ -416,9 +523,10 @@
         compiler_params=params(collective_id=1, has_side_effects=True),
         name="moe",
     )(
-        query, out_local, start, z_proj, head_gain.reshape(1, dim), residual,
-        post_gain.reshape(1, width), share, shared_gate.reshape(1, width), out_weight,
-        expert_gate_up, expert_down, shared_gate_up, shared_down,
+        flat_qk, v_proj, conv_qk, conv_v, decay_log, beta_gate, doc_ids.reshape(1, -1), route_ids,
+        route_weight, z_proj, head_gain.reshape(1, dim), residual, post_gain.reshape(1, width),
+        shared_gate.reshape(1, width), out_weight, expert_gate_up, expert_down, shared_gate_up,
+        shared_down,
     )
 
 
@@ -441,15 +549,23 @@
     me = place * lax.axis_size("exp") + lax.axis_index("exp")
     exp_dev = expert_down.shape[0]
 
+    experts_all = exp_dev * seq_count * lax.axis_size("exp")
+    flat_qk = qk_proj.reshape(length, 2 * key_cols)
+    if seq_count == 8 and lax.axis_size("exp") == 4 and 2 * experts_all == 128:
+        return moe_call(
+            flat_qk, v_proj, z_proj, conv_qk, conv_v, decay_log, beta_gate, doc_ids, head_gain,
+            out_weight, residual, post_gain, route_ids, route_weight, expert_gate_up, expert_down,
+            shared_gate_up, shared_down, shared_gate,
+        )
+
     own_share = jnp.sum(
         jnp.where(
-            route_ids[:, :, None] == jnp.arange(exp_dev * seq_count * lax.axis_size("exp")),
+            route_ids[:, :, None] == jnp.arange(experts_all),
             route_weight[:, :, None],
             0.0,
         ),
         axis=1,
     )
-    flat_qk = qk_proj.reshape(length, 2 * key_cols)
     rim = shifted(
         jnp.concatenate([flat_qk[length - RIM :], v_proj[length - RIM :]], axis=1), "seq", 1
     )
@@ -482,14 +598,6 @@
         before = shifted(state.astype(bf16), "seq", 1)
         state = add + jnp.einsum("hkl,hlv->hkv", move, before, preferred_element_type=f32)
     start = shifted(state.astype(bf16), "seq", 1)
-    if seq_count == 8 and lax.axis_size("exp") == 4 and 2 * own_share.shape[1] == 128:
-        rounded = own_share.astype(bf16)
-        rest = (own_share - rounded.astype(f32)).astype(bf16)
-        share = jnp.concatenate([rounded, rest], axis=1)
-        return moe_call(
-            query, out_local, start, z_proj, head_gain, residual, post_gain, share, shared_gate,
-            out_weight, expert_gate_up, expert_down, shared_gate_up, shared_down,
-        )
     shares = lax.all_gather(own_share, ("seq", "exp"), axis=0, tiled=True)
     shares = lax.dynamic_slice_in_dim(shares, me * exp_dev, exp_dev, axis=1)
     part = pl.pallas_call(

time: 138 us -> 108 us (0.78)
  Pallas kernels: 110 us -> 99 us
  starting transfers between devices: 9.7 us -> 0 us
  other arithmetic: 4 us -> 0 us
  local copies, waits for them, and re-layouts: 11 us -> 7.57 us
    pallas_call x1 -> x0, Pallas kernels: 16.9 us -> none  [shards(): pl.pallas_call(delta_kernel, out_shape=(jax.ShapeDtypeStruct((heads, leng...]
    ppermute x3 -> x0, starting transfers between devices: 9.7 us -> none  [shifted(): return lax.ppermute(value, axis, pairs)]
    pallas_call x1, Pallas kernels: 92.9 us -> 99 us  [moe_call(): pl.pallas_call(moe_kernel, out_shape=(row_block, row_block), in_specs=[VM...]
    unnamed x10 -> x5, local copies, waits for them, and re-layouts: 8.18 us -> 7.57 us
  transfers between devices with their start and end apart: 3 -> 0, of which waited for: 2 -> 0; matrix products, arithmetic and copies ran while one was open for 6% -> 0% of each run, Pallas kernels for 0% -> 0%
where the time goes in v3:
time: 108 us; the launch traced here: 107 us
  Pallas kernels  99 us (92%)
  local copies, waits for them, and re-layouts  7.57 us (7%)
    pallas_call x1, Pallas kernels, moe_call(): pl.pallas_call(moe_kernel, out_shape=(row_block, row_block), in_specs=[VM...  99 us
    unnamed x5, local copies, waits for them, and re-layouts  7.57 us

profile of v3, /device:TPU:24, one launch (start us, length us, event | category | flops | bytes accessed | tf_op | source)
XLA Modules:
  0.0 107.2 jit_solution(7086004194293618640)
XLA Ops:
  0.6 1.4 %copy.21.ids_ref = s32[32,10]{1,0:T(8,128)} copy(s32[32,10]{0,1:T(8,128)} %param.31) | data formatting | bytes 2560 | tf_op args[12]
  2.0 1.4 %copy.22.route_ref = f32[32,10]{1,0:T(8,128)} copy(f32[32,10]{0,1:T(8,128)} %param.32) | data formatting | bytes 2560 | tf_op args[13]
  3.4 1.7 %copy.23 = bf16[16,8,2,512]{3,1,2,0:T(8,128)(2,1)} copy(bf16[16,8,2,512]{3,2,1,0:T(2,128)(2,1)} %bitcast.7) | data formatting | bytes 524288
  5.1 99.0 %moe.1 = (bf16[32,2048]{1,0:T(8,128)(2,1)}, bf16[32,2048]{1,0:T(8,128)(2,1)}) custom-call(bf16[128,1024]{1,0:T(8,128)(2,1)} %bitcast.6, bf16[128,1024]{1,0:T(8,128)(2,1)} %v_ref.1, f32[4,2,512]{2,1,0:T(2,128)} %taps_qk_ref.1, f32[4,1024]{1,0:T(4,128)} %taps_v_ref.1, f32[8,128]{1,0:T(8,128)} %decay_ref.1, f32[8,128]{1,0:T(8,128)} %beta_ref.1, ...), custom_call_target="tpu_custom_call" | custom-call | tf_op jit(solution)/shard_map/moe/pallas_call | solution.py:478
  104.1 1.6 %copy.26 = bf16[32,2048]{1,0:T(8,128)(2,1)} copy(bf16[32,2048]{1,0:T(8,128)(2,1)} %get-tuple-element.4) | data formatting | bytes 262144
  105.7 1.6 %copy.27 = bf16[32,2048]{1,0:T(8,128)(2,1)} copy(bf16[32,2048]{1,0:T(8,128)(2,1)} %get-tuple-element.5) | data formatting | bytes 262144

commit v4 on v3

--- a/solution.py
+++ b/solution.py
@@ -319,9 +319,14 @@
     tok[0, :, 0:width] = normed
     lane = lax.broadcasted_iota(jnp.int32, (1, lanes), 1)
     named = lax.rem(lane, lanes // 2)
-    share = jnp.zeros((rows, lanes), f32)
-    for n in range(ids_ref.shape[1]):
-        share = share + jnp.where(ids_ref[:, n : n + 1] == named, route_ref[:, n : n + 1], 0.0)
+    expert = lax.rem(lax.broadcasted_iota(jnp.int32, (lanes, rows), 0), lanes // 2)
+    by_expert = jnp.zeros((lanes, rows), f32)
+    for n in range(ids_ref.shape[0]):
+        by_expert = by_expert + jnp.where(
+            ids_ref[n : n + 1, :] == expert, route_ref[n : n + 1, :], 0.0
+        )
+    diagonal = lax.broadcasted_iota(jnp.int32, (lanes, lanes), 0) == lane
+    share = dot_exact(by_expert, diagonal.astype(f32), ((0,), (0,)))
     rest = share - share.astype(bf16).astype(f32)
     tok[0, :, width:] = jnp.where(lane < lanes // 2, share, rest).astype(bf16)
 
@@ -411,22 +416,33 @@
         arrived(slot(3, 1, k))
     work(3)
     core_copies[3].wait()
-    send_x[2] = (mine[3, low, :] + core_recv[3, low, :]).astype(bf16)
-    by_x = send(send_x.at[2], pass_x, plane_sems, 2, to_x)
-    send_y[2] = (mine[3, high, :] + core_recv[3, high, :]).astype(bf16)
-    by_y = send(send_y.at[2], pass_y, plane_sems, 3, to_y)
+    order = list(range(1, depth)) + [0]
+    across, relays = {}, {}
+    for k in order:
+        at = pl.ds(k % middle * rows, rows)
+        block = slice(k * rows, (k + 1) * rows)
+        out, land, peer = (send_x, pass_x, to_x) if k < middle else (send_y, pass_y, to_y)
+        out[2, at, :] = (mine[3, block, :] + core_recv[3, block, :]).astype(bf16)
+        across[k] = send(out.at[2, at], land.at[at], plane_sems, 2 + k, peer)
     for k in range(depth):
         arrived(slot(0, 1, k))
     work(0)
     core_copies[0].wait()
     own = mine[0] + core_recv[0]
     mine[0] = own
-    by_x.wait()
-    send_y[0] = (mine[2, low, :] + core_recv[2, low, :] + pass_x[...].astype(f32)).astype(bf16)
-    plane.append(send(send_y.at[0], recv_y.at[0], plane_sems, 4, to_y))
-    by_y.wait()
-    send_x[1] = (mine[1, high, :] + core_recv[1, high, :] + pass_y[...].astype(f32)).astype(bf16)
-    plane.append(send(send_x.at[1], recv_x.at[1], plane_sems, 5, to_x))
+    for k in order:
+        at = pl.ds(k % middle * rows, rows)
+        block = slice(k * rows, (k + 1) * rows)
+        across[k].wait()
+        if k < middle:
+            passed = mine[2, block, :] + core_recv[2, block, :] + pass_x[at, :].astype(f32)
+            send_y[0, at, :] = passed.astype(bf16)
+            out, land, peer = send_y.at[0, at], recv_y.at[0, at], to_y
+        else:
+            passed = mine[1, block, :] + core_recv[1, block, :] + pass_y[at, :].astype(f32)
+            send_x[1, at, :] = passed.astype(bf16)
+            out, land, peer = send_x.at[1, at], recv_x.at[1, at], to_x
+        relays[k] = send(out, land, plane_sems, 2 + depth + k, peer)
     for copy in plane:
         copy.wait()
     back_copies = []
@@ -440,10 +456,12 @@
         )
 
     for k in range(1, depth):
+        relays[k].wait()
         back_send[k] = summed(k).astype(bf16)
         back_copies.append(
             send(back_send.at[k], back_recv.at[depth - k], back_sems, depth - k, ahead[k])
         )
+    relays[0].wait()
     normed = tok[0, :, 0:width]
     score = jax.nn.sigmoid(
         jnp.sum(normed.astype(f32) * gate_ref[...], axis=1, keepdims=True)
@@ -517,14 +535,14 @@
             dma((2, depth)),
             dma((2, 8 * depth)),
             dma((2, 4)),
-            dma((2, 6)),
+            dma((2, 2 + 2 * depth)),
             dma((2, depth)),
         ],
         compiler_params=params(collective_id=1, has_side_effects=True),
         name="moe",
     )(
-        flat_qk, v_proj, conv_qk, conv_v, decay_log, beta_gate, doc_ids.reshape(1, -1), route_ids,
-        route_weight, z_proj, head_gain.reshape(1, dim), residual, post_gain.reshape(1, width),
+        flat_qk, v_proj, conv_qk, conv_v, decay_log, beta_gate, doc_ids.reshape(1, -1), route_ids.T,
+        route_weight.T, z_proj, head_gain.reshape(1, dim), residual, post_gain.reshape(1, width),
         shared_gate.reshape(1, width), out_weight, expert_gate_up, expert_down, shared_gate_up,
         shared_down,
     )

time: 108 us -> 101 us (0.935)
  Pallas kernels: 99 us -> 95.2 us
  local copies, waits for them, and re-layouts: 7.57 us -> 4.82 us
    pallas_call x1, Pallas kernels: 99 us -> 95.2 us  [moe_call(): pl.pallas_call(moe_kernel, out_shape=(row_block, row_block), in_specs=[VM...]
    unnamed x5 -> x3, local copies, waits for them, and re-layouts: 7.57 us -> 4.82 us
where the time goes in v4:
time: 101 us
  Pallas kernels  95.2 us (94%)
  local copies, waits for them, and re-layouts  4.82 us (5%)
    pallas_call x1, Pallas kernels, moe_call(): pl.pallas_call(moe_kernel, out_shape=(row_block, row_block), in_specs=[VM...  95.2 us
    unnamed x3, local copies, waits for them, and re-layouts  4.82 us

profile of v4, /device:TPU:24, one launch (start us, length us, event | category | flops | bytes accessed | tf_op | source)
XLA Modules:
  0.0 100.7 jit_solution(10343028922490866803)
XLA Ops:
  0.6 1.7 %copy.21 = bf16[16,8,2,512]{3,1,2,0:T(8,128)(2,1)} copy(bf16[16,8,2,512]{3,2,1,0:T(2,128)(2,1)} %bitcast.9) | data formatting | bytes 524288
  2.3 95.2 %moe.1 = (bf16[32,2048]{1,0:T(8,128)(2,1)}, bf16[32,2048]{1,0:T(8,128)(2,1)}) custom-call(bf16[128,1024]{1,0:T(8,128)(2,1)} %bitcast.8, bf16[128,1024]{1,0:T(8,128)(2,1)} %v_ref.1, f32[4,2,512]{2,1,0:T(2,128)} %taps_qk_ref.1, f32[4,1024]{1,0:T(4,128)} %taps_v_ref.1, f32[8,128]{1,0:T(8,128)} %decay_ref.1, f32[8,128]{1,0:T(8,128)} %beta_ref.1, ...), custom_call_target="tpu_custom_call" | custom-call | tf_op jit(solution)/shard_map/moe/pallas_call | solution.py:496
  97.5 1.6 %copy.24 = bf16[32,2048]{1,0:T(8,128)(2,1)} copy(bf16[32,2048]{1,0:T(8,128)(2,1)} %get-tuple-element.4) | data formatting | bytes 262144
  99.1 1.6 %copy.25 = bf16[32,2048]{1,0:T(8,128)(2,1)} copy(bf16[32,2048]{1,0:T(8,128)(2,1)} %get-tuple-element.5) | data formatting | bytes 262144
